TPU v7x, 32 devices: a whole 2x2x4 slice. The times are simulated.
32 devices in a mesh: dp: 16 (over z, y, x), tensor: 2 (over core).
Axes of the slice: x: 2, y: 2, z: 4, core: 2. Of those that a mesh axis runs over, the one named last changes fastest.
Arguments:
- layer_input: bfloat16 [20480, 1536], P('dp'), may hold values from -6 to 6
- branch_point: int32 [16, 2], P('dp'), may hold values from 512 to 1024, as said below
- attn_gain: float32 [1536], replicated, may hold values from 0.5 to 1.5
- w_query: bfloat16 [1536, 1536], P(None, 'tensor'), may hold values from -0.15625 to 0.15625
- w_key: bfloat16 [1536, 768], P(None, 'tensor'), may hold values from -0.15625 to 0.15625
- w_value: bfloat16 [1536, 768], P(None, 'tensor'), may hold values from -0.15625 to 0.15625
- w_out: bfloat16 [1536, 1536], P('tensor'), may hold values from -0.875 to 0.875
- ffn_gain: float32 [1536], replicated, may hold values from 0.5 to 1.5
- w_gate: bfloat16 [1536, 4096], P(None, 'tensor'), may hold values from -0.15625 to 0.15625
- w_up: bfloat16 [1536, 4096], P(None, 'tensor'), may hold values from -0.15625 to 0.15625
- w_down: bfloat16 [4096, 1536], P('tensor'), may hold values from -0.09375 to 0.09375
- cotangent: bfloat16 [20480, 1536], P('dp'), may hold values from -6 to 6
Outputs:
- output: bfloat16 [20480, 1536], P('dp')
- grad_input: bfloat16 [20480, 1536], P('dp')
- grad_attn_gain: float32 [1536], P('dp')
- grad_query: float32 [1536, 1536], P('dp', 'tensor')
- grad_key: float32 [1536, 768], P('dp', 'tensor')
- grad_value: float32 [1536, 768], P('dp', 'tensor')
- grad_out_proj: float32 [1536, 1536], P('tensor', 'dp')
- grad_ffn_gain: float32 [1536], P('dp')
- grad_gate: float32 [1536, 4096], P('dp', 'tensor')
- grad_up: float32 [1536, 4096], P('dp', 'tensor')
- grad_down: float32 [4096, 1536], P('tensor', 'dp')
Inputs may be any that keep to these rules, and one draw needn't show every extreme that they name: `branch_point`: in every group one continuation follows the whole prompt; every continuation follows 1024 // 2 prompt tokens or more.
All inputs are finite; a program needn't handle non-finite values.
Results may differ from a plain program's by a relative error of at most 0.017.
Values may be sent and summed in bfloat16 or wider, within the bound.
No kernel may reach another device: no remote copies, remote signals or barrier semaphores. Data moves between devices by JAX's collectives and lax.ppermute only.
A program may use at most 320 MiB of HBM per device.

v0:
```python
import jax
import jax.numpy as jnp
from jax import lax
from jax.sharding import PartitionSpec as P

HEAD_DIM = 96
PROMPT = 1024
CONT_LEN = 128
CONT = 2
GROUP_TOK = 1280


epsilon = 1e-05
rope_base = 100000.0


def rms_norm(values, scale_gain):
    return (
        values * lax.rsqrt(jnp.mean(values * values, axis=-1, keepdims=True) + epsilon) * scale_gain
    )


def group_layout(branch):
    row_ids = jnp.arange(GROUP_TOK, dtype=jnp.int32)
    cont_ids = jnp.arange(CONT, dtype=jnp.int32)
    owners = jnp.concatenate([jnp.full((PROMPT,), -1, jnp.int32), jnp.repeat(cont_ids, CONT_LEN)])
    reaches = jnp.sum(jnp.where(owners[:, None] == cont_ids[None, :], branch[None, :], 0), axis=1)
    offset = jnp.maximum(row_ids - PROMPT, 0) % CONT_LEN
    positions = jnp.where(owners < 0, row_ids, reaches + offset)
    own_block = (owners[:, None] == owners[None, :]) & (row_ids[None, :] <= row_ids[:, None])
    into_prompt = (
        (owners[None, :] < 0) & (owners[:, None] >= 0) & (row_ids[None, :] < reaches[:, None])
    )
    return (positions, own_block | into_prompt)


def rotary(tensor, positions):
    half_dim = tensor.shape[-1] // 2
    frequency = rope_base ** (-jnp.arange(half_dim, dtype=jnp.float32) * 2.0 / tensor.shape[-1])
    angles = positions.astype(jnp.float32)[:, None] * frequency[None, :]
    cosine = jnp.cos(angles)[:, None, :]
    sine_part = jnp.sin(angles)[:, None, :]
    leading = tensor[..., :half_dim]
    trailing = tensor[..., half_dim:]
    return jnp.concatenate(
        [leading * cosine - trailing * sine_part, trailing * cosine + leading * sine_part], axis=-1
    )


def block_scores(query_block, allowed_block, keys):
    scores = jnp.einsum(
        "qkgd,pkd->kgqp", query_block, keys, preferred_element_type=jnp.float32
    ) * HEAD_DIM ** (-0.5)
    return jnp.where(allowed_block[None, None], scores, -1e30)


def swiglu(gate, up_proj):
    return jax.nn.silu(gate) * up_proj


def per_device(
    layer_input,
    branch_point,
    attn_gain,
    w_query,
    w_key,
    w_value,
    w_out,
    ffn_gain,
    w_gate,
    w_up,
    w_down,
    cotangent,
):
    positions, allowed = group_layout(branch_point[0])
    local_heads = w_query.shape[1] // HEAD_DIM
    local_kv = w_key.shape[1] // HEAD_DIM
    grouping = local_heads // local_kv
    block_rows = GROUP_TOK // 2
    scale = HEAD_DIM ** (-0.5)
    inputs = layer_input.astype(jnp.float32)
    grad_out = cotangent.astype(jnp.float32)
    normed_one, pull_one = jax.vjp(rms_norm, inputs, attn_gain)
    act_one = normed_one.astype(jnp.bfloat16)
    query_lin = jnp.dot(act_one, w_query, preferred_element_type=jnp.float32).reshape(
        GROUP_TOK, local_heads, HEAD_DIM
    )
    key_lin = jnp.dot(act_one, w_key, preferred_element_type=jnp.float32).reshape(
        GROUP_TOK, local_kv, HEAD_DIM
    )
    value_lin = jnp.dot(act_one, w_value, preferred_element_type=jnp.float32).reshape(
        GROUP_TOK, local_kv, HEAD_DIM
    )
    queries = (
        rotary(query_lin, positions)
        .astype(jnp.bfloat16)
        .reshape(2, block_rows, local_kv, grouping, HEAD_DIM)
    )
    keys = rotary(key_lin, positions).astype(jnp.bfloat16)
    values = value_lin.astype(jnp.bfloat16)
    allowed_blocks = allowed.reshape(2, block_rows, GROUP_TOK)

    def forward_block(item):
        scores = block_scores(item[0], item[1], keys)
        largest = jnp.max(scores, axis=-1, keepdims=True)
        shifted = jnp.exp(scores - largest)
        totals = jnp.sum(shifted, axis=-1, keepdims=True)
        probs = (shifted / totals).astype(jnp.bfloat16)
        result = jnp.einsum("kgqp,pkd->qkgd", probs, values, preferred_element_type=jnp.float32)
        return (result, (largest + jnp.log(totals))[..., 0])

    mixed, log_totals = lax.map(forward_block, (queries, allowed_blocks))
    mixed = mixed.reshape(GROUP_TOK, local_heads * HEAD_DIM).astype(jnp.bfloat16)
    partial_attn = jnp.dot(mixed, w_out, preferred_element_type=jnp.float32)
    hidden_state = inputs + lax.psum(partial_attn.astype(jnp.bfloat16), "tensor").astype(
        jnp.float32
    )
    normed_two, pull_two = jax.vjp(rms_norm, hidden_state, ffn_gain)
    act_two = normed_two.astype(jnp.bfloat16)
    gate = jnp.dot(act_two, w_gate, preferred_element_type=jnp.float32)
    up_proj = jnp.dot(act_two, w_up, preferred_element_type=jnp.float32)
    units_full, pull_units = jax.vjp(swiglu, gate, up_proj)
    hidden_units = units_full.astype(jnp.bfloat16)
    partial_ffn = jnp.dot(hidden_units, w_down, preferred_element_type=jnp.float32)
    output = (
        hidden_state + lax.psum(partial_ffn.astype(jnp.bfloat16), "tensor").astype(jnp.float32)
    ).astype(jnp.bfloat16)
    grad_down_w = jnp.einsum(
        "tf,td->fd", hidden_units, cotangent, preferred_element_type=jnp.float32
    )
    grad_units = jnp.einsum("td,fd->tf", cotangent, w_down, preferred_element_type=jnp.float32)
    grad_gate_full, grad_up_full = pull_units(grad_units)
    grad_gate_lin = grad_gate_full.astype(jnp.bfloat16)
    grad_up_lin = grad_up_full.astype(jnp.bfloat16)
    grad_gate_w = jnp.einsum(
        "td,tf->df", act_two, grad_gate_lin, preferred_element_type=jnp.float32
    )
    grad_up_w = jnp.einsum("td,tf->df", act_two, grad_up_lin, preferred_element_type=jnp.float32)
    partial_two = jnp.einsum("tf,df->td", grad_gate_lin, w_gate, preferred_element_type=jnp.float32)
    partial_two = partial_two + jnp.einsum(
        "tf,df->td", grad_up_lin, w_up, preferred_element_type=jnp.float32
    )
    grad_act_two = lax.psum(partial_two.astype(jnp.bfloat16), "tensor").astype(jnp.float32)
    grad_from_two, grad_ffn_gain = pull_two(grad_act_two)
    grad_hidden = grad_out + grad_from_two
    grad_attention = grad_hidden.astype(jnp.bfloat16)
    grad_out_w = jnp.einsum("tc,td->cd", mixed, grad_attention, preferred_element_type=jnp.float32)
    grad_mixed = jnp.einsum(
        "td,cd->tc", grad_attention, w_out, preferred_element_type=jnp.float32
    ).astype(jnp.bfloat16)
    grad_mixed = grad_mixed.reshape(2, block_rows, local_kv, grouping, HEAD_DIM)

    def backward_block(carry, item):
        key_grads, value_grads = carry
        query_block, allowed_block, grad_block, block_totals = item
        scores = block_scores(query_block, allowed_block, keys)
        probs_full = jnp.exp(scores - block_totals[..., None])
        grad_probs = jnp.einsum(
            "qkgd,pkd->kgqp", grad_block, values, preferred_element_type=jnp.float32
        )
        weighted = jnp.sum(probs_full * grad_probs, axis=-1, keepdims=True)
        grad_scores = (probs_full * (grad_probs - weighted)).astype(jnp.bfloat16)
        query_grad = (
            jnp.einsum("kgqp,pkd->qkgd", grad_scores, keys, preferred_element_type=jnp.float32)
            * scale
        )
        key_grads = (
            key_grads
            + jnp.einsum(
                "kgqp,qkgd->pkd", grad_scores, query_block, preferred_element_type=jnp.float32
            )
            * scale
        )
        value_grads = value_grads + jnp.einsum(
            "kgqp,qkgd->pkd",
            probs_full.astype(jnp.bfloat16),
            grad_block,
            preferred_element_type=jnp.float32,
        )
        return ((key_grads, value_grads), query_grad)

    empty = jnp.zeros((GROUP_TOK, local_kv, HEAD_DIM), jnp.float32)
    (key_grads, value_grads), query_grads = lax.scan(
        backward_block, (empty, empty), (queries, allowed_blocks, grad_mixed, log_totals)
    )
    back_positions = -positions
    grad_query_lin = rotary(query_grads.reshape(GROUP_TOK, local_heads, HEAD_DIM), back_positions)
    grad_query_lin = grad_query_lin.reshape(GROUP_TOK, local_heads * HEAD_DIM).astype(jnp.bfloat16)
    grad_key_lin = (
        rotary(key_grads, back_positions)
        .reshape(GROUP_TOK, local_kv * HEAD_DIM)
        .astype(jnp.bfloat16)
    )
    grad_value_lin = value_grads.reshape(GROUP_TOK, local_kv * HEAD_DIM).astype(jnp.bfloat16)
    grad_query_w = jnp.einsum(
        "td,tc->dc", act_one, grad_query_lin, preferred_element_type=jnp.float32
    )
    grad_key_w = jnp.einsum("td,tc->dc", act_one, grad_key_lin, preferred_element_type=jnp.float32)
    grad_value_w = jnp.einsum(
        "td,tc->dc", act_one, grad_value_lin, preferred_element_type=jnp.float32
    )
    partial_one = jnp.einsum(
        "tc,dc->td", grad_query_lin, w_query, preferred_element_type=jnp.float32
    )
    partial_one = partial_one + jnp.einsum(
        "tc,dc->td", grad_key_lin, w_key, preferred_element_type=jnp.float32
    )
    partial_one = partial_one + jnp.einsum(
        "tc,dc->td", grad_value_lin, w_value, preferred_element_type=jnp.float32
    )
    grad_act_one = lax.psum(partial_one.astype(jnp.bfloat16), "tensor").astype(jnp.float32)
    grad_from_one, grad_attn_gain = pull_one(grad_act_one)
    grad_input = (grad_hidden + grad_from_one).astype(jnp.bfloat16)
    summed = (
        lax.psum_scatter(grad_attn_gain, "dp", scatter_dimension=0, tiled=True),
        lax.psum_scatter(grad_query_w, "dp", scatter_dimension=0, tiled=True),
        lax.psum_scatter(grad_key_w, "dp", scatter_dimension=0, tiled=True),
        lax.psum_scatter(grad_value_w, "dp", scatter_dimension=0, tiled=True),
        lax.psum_scatter(grad_out_w, "dp", scatter_dimension=1, tiled=True),
        lax.psum_scatter(grad_ffn_gain, "dp", scatter_dimension=0, tiled=True),
        lax.psum_scatter(grad_gate_w, "dp", scatter_dimension=0, tiled=True),
        lax.psum_scatter(grad_up_w, "dp", scatter_dimension=0, tiled=True),
        lax.psum_scatter(grad_down_w, "dp", scatter_dimension=1, tiled=True),
    )
    return (
        output,
        grad_input,
        summed[0],
        summed[1],
        summed[2],
        summed[3],
        summed[4],
        summed[5],
        summed[6],
        summed[7],
        summed[8],
    )


def solution(mesh):
    placed = (
        P("dp", None),
        P("dp", None),
        P(),
        P(None, "tensor"),
        P(None, "tensor"),
        P(None, "tensor"),
        P("tensor", None),
        P(),
        P(None, "tensor"),
        P(None, "tensor"),
        P("tensor", None),
        P("dp", None),
    )
    return jax.shard_map(
        per_device,
        mesh=mesh,
        in_specs=placed,
        out_specs=(
            P("dp", None),
            P("dp", None),
            P("dp"),
            P("dp", "tensor"),
            P("dp", "tensor"),
            P("dp", "tensor"),
            P("tensor", "dp"),
            P("dp"),
            P("dp", "tensor"),
            P("dp", "tensor"),
            P("tensor", "dp"),
        ),
        check_vma=False,
    )
```

profile of v0, /device:TPU:0, one launch (start us, length us, event | category | flops | bytes accessed | tf_op | source)
XLA Modules:
  0.0 1814.5 jit_solution(1668633604226079758)
XLA Ops:
  52.0 82.6 %while.27 = (s32[]{:T(128)}, bf16[2,640,4,2,96]{1,4,3,2,0:T(8,128)(2,1)}, f32[2,4,2,640]{3,2,1,0:T(2,128)}, pred[2,640,1280]{2,1,0:T(8,128)(4,1)}, bf16[2,640,4,...) while((s32[]{:T(128)}, ...), condition=%wide.region_5.6_spmd, body=%wide.region_2.5_spmd.sunk | while | flops 2595220480 | bytes 88147088 | solution.py:112
  145.0 27.5 %all-reduce.9.cloned.1.call-done = bf16[1280,1536]{1,0:T(8,128)(2,1)} async-done(((bf16[1280,1536]{1,0:T(8,128)(2,1)}), bf16[1280,1536]{1,0:T(8,128)(2,1)}) %all-reduce.9.cloned.1.call-update) | async-done | bytes 3932176 | tf_op jit(solution)/shard_map/psum | solution.py:115
  201.9 23.4 %multiply_convert_fusion = (bf16[1280,2048]{1,0:T(8,128)(2,1)}, bf16[1280,2048]{1,0:T(8,128)(2,1)}, bf16[1280,2048]{1,0:T(8,128)(2,1)}) fusion(f32[1280,2048]{1,0:T(8,128)} %fusion.89, f32[1280,2048]{1,0:T(8,128)} %fusion.90, bf16[1280,1536]{1,0:T(8,128)(2,1)} %param.27, bf16[2048,1536]{1,0:T(8,128)(2,1)} %param.26), kind=kOutput, calls=%fused_computation.63 | convolution fusion | flops 8095006720 | bytes 46923776 | tf_op jit(solution)/shard_map/td,fd->tf/dot_general | solution.py:131
  308.8 259.7 %while.28 = (s32[]{:T(128)}, f32[1280,4,96]{0,2,1:T(8,128)}, f32[1280,4,96]{0,2,1:T(8,128)}, f32[2,640,4,2,96]{1,0,4,3,2:T(2,128)}, bf16[2,640,4,2,96]{1,4,3,2,0...) while((s32[]{:T(128)}, f32[1280,4,96]{0,2,1:T(8,128)}, ...), condition=%wide.region_13.14_spmd.clone, body=%wide.region_11.13_spmd.clone.sunk | while | flops 6353382400 | bytes 253892368 | solution.py:183
  309.0 13.9 fusion.157
  323.0 20.1 %fusion.158 = (f32[4,2,640]{2,1,0:T(2,128)S(1)}, f32[4,2,640,1280]{3,2,1,0:T(8,128)}) fusion(f32[4,640,2,1280]{3,1,2,0:T(8,128)} %fusion.157, f32[4,2,640]{2,1,0:T(2,128)S(1)} %dynamic-slice_bitcast_fusion.7, bf16[1280,4,96]{0,2,1:T(8,128)(2,1)S(1)} %get-tuple-element.437, bf16[2,640,4,2,96]{1,4,3,2,0:T(8,128)(2,1)S(1)} %copy-done.9, ...), kind=kOutput, calls=%fused_computation.20.clone.1 | convolution fusion | flops 1291054080 | bytes 55255044 | tf_op jit(solution)/shard_map/while/body/eval_jaxpr/qkgd,pkd->kgqp/dot_general | solution.py:51
  343.1 21.9 %fusion.159 = bf16[4,2,640,1280]{3,2,1,0:T(8,128)(2,1)} fusion(f32[4,2,640,1280]{3,2,1,0:T(8,128)} %get-tuple-element.381, f32[4,640,2,1280]{3,1,2,0:T(8,128)} %fusion.157, f32[4,2,640]{2,1,0:T(2,128)S(1)} %get-tuple-element.382), kind=kLoop, calls=%fused_computation.22.clone.1 | loop fusion | flops 19660800 | bytes 65556480 | tf_op jit(solution)/shard_map/while/body/eval_jaxpr/convert_element_type | solution.py:162
  378.6 38.4 %dynamic_update_slice.19 = f32[2,640,4,2,96]{1,0,4,3,2:T(2,128)} dynamic-update-slice(f32[2,640,4,2,96]{1,0,4,3,2:T(2,128)} %get-tuple-element.422, f32[1,640,4,2,96]{1,0,4,3,2:T(1,128)S(1)} %copy.62, s32[]{:T(128)} %get-tuple-element.419, s32[]{:T(128)} %constant.79.clone.1..sunk, s32[]{:T(128)} %constant.79.clone.1..sunk, s32[]{:T(128)} %constant.79.clone.1..sunk, s32[]{:T(128)} %constant.79.clone.1..sunk) | dynamic-update-slice | bytes 3932164 | tf_op jit(solution)/shard_map/while/body/jit(dynamic_update_index_in_dim)/dynamic_update_slice | solution.py:112
  438.4 13.9 fusion.157
  452.4 20.1 %fusion.158 = (f32[4,2,640]{2,1,0:T(2,128)S(1)}, f32[4,2,640,1280]{3,2,1,0:T(8,128)}) fusion(f32[4,640,2,1280]{3,1,2,0:T(8,128)} %fusion.157, f32[4,2,640]{2,1,0:T(2,128)S(1)} %dynamic-slice_bitcast_fusion.7, bf16[1280,4,96]{0,2,1:T(8,128)(2,1)S(1)} %get-tuple-element.437, bf16[2,640,4,2,96]{1,4,3,2,0:T(8,128)(2,1)S(1)} %copy-done.9, ...), kind=kOutput, calls=%fused_computation.20.clone.1 | convolution fusion | flops 1291054080 | bytes 55255044 | tf_op jit(solution)/shard_map/while/body/eval_jaxpr/qkgd,pkd->kgqp/dot_general | solution.py:51
  472.5 21.9 %fusion.159 = bf16[4,2,640,1280]{3,2,1,0:T(8,128)(2,1)} fusion(f32[4,2,640,1280]{3,2,1,0:T(8,128)} %get-tuple-element.381, f32[4,640,2,1280]{3,1,2,0:T(8,128)} %fusion.157, f32[4,2,640]{2,1,0:T(2,128)S(1)} %get-tuple-element.382), kind=kLoop, calls=%fused_computation.22.clone.1 | loop fusion | flops 19660800 | bytes 65556480 | tf_op jit(solution)/shard_map/while/body/eval_jaxpr/convert_element_type | solution.py:162
  508.0 38.4 %dynamic_update_slice.19 = f32[2,640,4,2,96]{1,0,4,3,2:T(2,128)} dynamic-update-slice(f32[2,640,4,2,96]{1,0,4,3,2:T(2,128)} %get-tuple-element.422, f32[1,640,4,2,96]{1,0,4,3,2:T(1,128)S(1)} %copy.62, s32[]{:T(128)} %get-tuple-element.419, s32[]{:T(128)} %constant.79.clone.1..sunk, s32[]{:T(128)} %constant.79.clone.1..sunk, s32[]{:T(128)} %constant.79.clone.1..sunk, s32[]{:T(128)} %constant.79.clone.1..sunk) | dynamic-update-slice | bytes 3932164 | tf_op jit(solution)/shard_map/while/body/jit(dynamic_update_index_in_dim)/dynamic_update_slice | solution.py:112
  603.3 14.1 fusion.64
  626.8 14.2 fusion.93
  641.1 14.1 fusion.94
  655.5 14.4 fusion.95
  677.2 77.4 %all-reduce.3 = (f32[1536]{0:T(1024)S(1)}, f32[1536]{0:T(1024)S(1)}) all-reduce(f32[1536]{0:T(1024)S(1)} %get-tuple-element.204, f32[1536]{0:T(1024)S(1)} %copy-done.39), channel_id=2, replica_groups=mesh['dp'=16,'tensor'=2] {'dp'}, use_global_device_ids=true, to_apply=%region_17.18.clone | all-reduce | flops 3072 | bytes 24576
  755.8 14.3 fusion.56
  770.1 122.8 %reduce-scatter.12.cloned.1.call-done = f32[96,384]{1,0:T(8,128)} async-done(((f32[1536,384]{1,0:T(8,128)}), f32[96,384]{1,0:T(8,128)}) %reduce-scatter.12.cloned.1.call-update) | async-done | bytes 147472 | tf_op jit(solution)/shard_map/reduce_scatter | solution.py:218
  892.9 142.0 %reduce-scatter.14.cloned.1.call-done = f32[768,96]{0,1:T(8,128)} async-done(((f32[768,1536]{0,1:T(8,128)}), f32[768,96]{0,1:T(8,128)}) %reduce-scatter.14.cloned.1.call-update) | async-done | bytes 294928 | tf_op jit(solution)/shard_map/reduce_scatter | solution.py:219
  1034.9 141.8 %reduce-scatter.8.cloned.1.call-done = f32[96,768]{1,0:T(8,128)} async-done(((f32[1536,768]{1,0:T(8,128)}), f32[96,768]{1,0:T(8,128)}) %reduce-scatter.8.cloned.1.call-update) | async-done | bytes 294928 | tf_op jit(solution)/shard_map/reduce_scatter | solution.py:216
  1176.7 210.2 %reduce-scatter.16.cloned.1.call-done = f32[96,2048]{1,0:T(8,128)} async-done(((f32[1536,2048]{1,0:T(8,128)}), f32[96,2048]{1,0:T(8,128)}) %reduce-scatter.16.cloned.1.call-update) | async-done | bytes 786448 | tf_op jit(solution)/shard_map/reduce_scatter | solution.py:221
  1386.9 209.9 %reduce-scatter.18.cloned.1.call-done = f32[96,2048]{1,0:T(8,128)} async-done(((f32[1536,2048]{1,0:T(8,128)}), f32[96,2048]{1,0:T(8,128)}) %reduce-scatter.18.cloned.1.call-update) | async-done | bytes 786448 | tf_op jit(solution)/shard_map/reduce_scatter | solution.py:222
  1596.8 210.7 %reduce-scatter.20.cloned.1.call-done = f32[2048,96]{0,1:T(8,128)} async-done(((f32[2048,1536]{0,1:T(8,128)}), f32[2048,96]{0,1:T(8,128)}) %reduce-scatter.20.cloned.1.call-update) | async-done | bytes 786448 | tf_op jit(solution)/shard_map/reduce_scatter | solution.py:223
  (221 shorter events, 372.8 us)
Async XLA Ops:
  7.2 132.6 %copy-start = (bf16[768,1536]{1,0:T(8,128)(2,1)S(1)}, bf16[768,1536]{1,0:T(8,128)(2,1)}, u32[]{:S(2)}) copy-start(bf16[768,1536]{1,0:T(8,128)(2,1)} %param.22) | copy-start | bytes 7077892
  7.2 165.3 %all-reduce.9.cloned.1.call-start = ((), (), s32[]{:S(2)}) async-start(), calls=%async_computation.7 | async-start | bytes 7864320 | tf_op jit(solution)/shard_map/psum | solution.py:115
  13.6 27.3 %copy-start.35 = (f32[1280]{0:T(1024)}, f32[1280]{0:T(1024)S(1)}, u32[]{:S(2)}) copy-start(f32[1280]{0:T(1024)S(1)} %fusion.73) | copy-start | bytes 15364
  66.4 13.3 copy-start.28
  79.7 13.6 copy-start.29
  120.9 13.6 copy-start.29
  144.9 32.4 %copy-start.37 = (f32[1536]{0:T(1024)S(1)}, f32[1536]{0:T(1024)}, u32[]{:S(2)}) copy-start(f32[1536]{0:T(1024)} %param.23) | copy-start | bytes 18436
  144.9 130.9 %all-reduce.11.cloned.1.call-start = ((), (), s32[]{:S(2)}) async-start(), calls=%async_computation.8 | async-start | bytes 7864320 | tf_op jit(solution)/shard_map/psum | solution.py:143
  178.1 105.9 %copy-start.31 = (f32[1280]{0:T(1024)}, f32[1280]{0:T(1024)S(1)}, u32[]{:S(2)}) copy-start(f32[1280]{0:T(1024)S(1)} %fusion.74) | copy-start | bytes 15364
  249.8 422.1 %all-reduce.13.cloned.1.call-start = ((), (), s32[]{:S(2)}) async-start(), calls=%async_computation.16 | async-start | bytes 15728640 | tf_op jit(solution)/shard_map/psum | solution.py:126
  293.4 15.4 copy-start.30
  309.0 13.9 copy-start.12
  309.0 14.0 copy-start.9
  438.4 13.9 copy-start.12
  438.4 14.0 copy-start.9
  589.3 180.8 %reduce-scatter.10.cloned.1.call-start = ((), (), s32[]{:S(2)}) async-start(), calls=%async_computation.10 | async-start | bytes 2506752 | tf_op jit(solution)/shard_map/reduce_scatter | solution.py:217
  596.2 296.8 %reduce-scatter.12.cloned.1.call-start = ((), (), s32[]{:S(2)}) async-start(), calls=%async_computation.11 | async-start | bytes 2506752 | tf_op jit(solution)/shard_map/reduce_scatter | solution.py:218
  603.2 431.7 %reduce-scatter.14.cloned.1.call-start = ((), (), s32[]{:S(2)}) async-start(), calls=%async_computation.12 | async-start | bytes 5013504 | tf_op jit(solution)/shard_map/reduce_scatter | solution.py:219
  617.4 559.3 %reduce-scatter.8.cloned.1.call-start = ((), (), s32[]{:S(2)}) async-start(), calls=%async_computation.9 | async-start | bytes 5013504 | tf_op jit(solution)/shard_map/reduce_scatter | solution.py:216
  626.8 760.1 %reduce-scatter.16.cloned.1.call-start = ((), (), s32[]{:S(2)}) async-start(), calls=%async_computation.13 | async-start | bytes 13369344 | tf_op jit(solution)/shard_map/reduce_scatter | solution.py:221
  641.0 955.7 %reduce-scatter.18.cloned.1.call-start = ((), (), s32[]{:S(2)}) async-start(), calls=%async_computation.14 | async-start | bytes 13369344 | tf_op jit(solution)/shard_map/reduce_scatter | solution.py:222
  655.2 1152.2 %reduce-scatter.20.cloned.1.call-start = ((), (), s32[]{:S(2)}) async-start(), calls=%async_computation.15 | async-start | bytes 13369344 | tf_op jit(solution)/shard_map/reduce_scatter | solution.py:223
  670.0 85.8 %copy-start.34 = (f32[1280]{0:T(1024)S(1)}, f32[1280]{0:T(1024)}, u32[]{:S(2)}) copy-start(f32[1280]{0:T(1024)} %copy-done.33) | copy-start | bytes 15364
  755.8 1051.7 %copy-start.1 = (bf16[768,1536]{1,0:T(8,128)(2,1)S(1)}, bf16[768,1536]{1,0:T(8,128)(2,1)}, u32[]{:S(2)}) copy-start(bf16[768,1536]{1,0:T(8,128)(2,1)} %param.22) | copy-start | bytes 7077892
  (42 other events, 236.4 us)
Sparse Core Ops, SparseCore 0:
  145.0 27.4 all-reduce.8
  249.9 25.9 all-reduce.10
  589.4 36.2 all-reduce.12
  631.8 128.9 reduce-scatter.9
  766.2 126.7 reduce-scatter.11
  899.4 135.4 reduce-scatter.13
  1040.6 136.0 reduce-scatter.7
  1183.9 202.9 reduce-scatter.15
  1393.1 203.6 reduce-scatter.17
  1603.8 203.6 reduce-scatter.19
where the time goes:
time: 1830 us; the launch traced here: 1810 us
  waiting for transfers between devices  1080 us (59%)
  matrix products  383 us (21%)
  local copies, waits for them, and re-layouts  131 us (7%)
  other arithmetic  129 us (7%)
  blocking collectives  77.4 us (4%)
    reduce_scatter x1, waiting for transfers between devices, per_device(): lax.psum_scatter(grad_down_w, 'dp', scatter_dimension=1, tiled=True)  211 us
    reduce_scatter x1, waiting for transfers between devices, per_device(): lax.psum_scatter(grad_gate_w, 'dp', scatter_dimension=0, tiled=True)  210 us
    reduce_scatter x1, waiting for transfers between devices, per_device(): lax.psum_scatter(grad_up_w, 'dp', scatter_dimension=0, tiled=True)  210 us
    reduce_scatter x1, waiting for transfers between devices, per_device(): lax.psum_scatter(grad_out_w, 'dp', scatter_dimension=1, tiled=True)  142 us
    reduce_scatter x1, waiting for transfers between devices, per_device(): lax.psum_scatter(grad_query_w, 'dp', scatter_dimension=0, tiled=True)  142 us
    reduce_scatter x1, waiting for transfers between devices, per_device(): lax.psum_scatter(grad_value_w, 'dp', scatter_dimension=0, tiled=True)  123 us
    dynamic_update_slice x4, local copies, waits for them, and re-layouts, per_device(): mixed, log_totals = lax.map(forward_block, (queries, allowed_blocks))  84 us
    unnamed x1, blocking collectives  77.4 us
  transfers between devices with their start and end apart: 10, of which 8 were waited for; matrix products, arithmetic and copies ran while one was open for 6% of the time, Pallas kernels for 0%

commit v1 on v0

--- a/solution.py
+++ b/solution.py
@@ -56,6 +56,37 @@
 
 def swiglu(gate, up_proj):
     return jax.nn.silu(gate) * up_proj
+
+
+def exchange_sum(partial):
+    sent = partial.astype(jnp.bfloat16)
+    received = lax.ppermute(sent, "tensor", [(0, 1), (1, 0)])
+    return sent.astype(jnp.float32) + received.astype(jnp.float32)
+
+
+def scatter_sum(grads, order):
+    size = lax.axis_size("dp")
+    bits = size.bit_length() - 1
+    me = lax.axis_index("dp")
+    work = grads.astype(jnp.bfloat16)
+    rows, width = work.shape
+    work = work.reshape((2,) * bits + (rows // size, width))
+    left = list(range(bits))[::-1]
+    for bit in [b for b in order if b < bits] + list(range(len(order), bits)):
+        axis = left.index(bit)
+        mine = (me >> bit) & 1
+        sent = lax.dynamic_index_in_dim(work, 1 - mine, axis, keepdims=False)
+        kept = lax.dynamic_index_in_dim(work, mine, axis, keepdims=False)
+        pairs = [(i, i ^ (1 << bit)) for i in range(size)]
+        received = lax.ppermute(sent, "dp", pairs)
+        total = kept.astype(jnp.float32) + received.astype(jnp.float32)
+        left.pop(axis)
+        work = total.astype(jnp.bfloat16) if left else total
+    return work
+
+
+X_FIRST = (0, 1, 2, 3)
+Y_FIRST = (1, 0, 2, 3)
 
 
 def per_device(
@@ -112,9 +143,7 @@
     mixed, log_totals = lax.map(forward_block, (queries, allowed_blocks))
     mixed = mixed.reshape(GROUP_TOK, local_heads * HEAD_DIM).astype(jnp.bfloat16)
     partial_attn = jnp.dot(mixed, w_out, preferred_element_type=jnp.float32)
-    hidden_state = inputs + lax.psum(partial_attn.astype(jnp.bfloat16), "tensor").astype(
-        jnp.float32
-    )
+    hidden_state = inputs + exchange_sum(partial_attn)
     normed_two, pull_two = jax.vjp(rms_norm, hidden_state, ffn_gain)
     act_two = normed_two.astype(jnp.bfloat16)
     gate = jnp.dot(act_two, w_gate, preferred_element_type=jnp.float32)
@@ -122,12 +151,17 @@
     units_full, pull_units = jax.vjp(swiglu, gate, up_proj)
     hidden_units = units_full.astype(jnp.bfloat16)
     partial_ffn = jnp.dot(hidden_units, w_down, preferred_element_type=jnp.float32)
-    output = (
-        hidden_state + lax.psum(partial_ffn.astype(jnp.bfloat16), "tensor").astype(jnp.float32)
-    ).astype(jnp.bfloat16)
-    grad_down_w = jnp.einsum(
-        "tf,td->fd", hidden_units, cotangent, preferred_element_type=jnp.float32
-    )
+    output = (hidden_state + exchange_sum(partial_ffn)).astype(jnp.bfloat16)
+    half = hidden_units.shape[1] // 2
+    grad_down_a, grad_down_b = [
+        scatter_sum(
+            jnp.einsum("td,tf->df", cotangent, part, preferred_element_type=jnp.float32), order
+        )
+        for part, order in (
+            (hidden_units[:, :half], X_FIRST),
+            (hidden_units[:, half:], Y_FIRST),
+        )
+    ]
     grad_units = jnp.einsum("td,fd->tf", cotangent, w_down, preferred_element_type=jnp.float32)
     grad_gate_full, grad_up_full = pull_units(grad_units)
     grad_gate_lin = grad_gate_full.astype(jnp.bfloat16)
@@ -140,11 +174,11 @@
     partial_two = partial_two + jnp.einsum(
         "tf,df->td", grad_up_lin, w_up, preferred_element_type=jnp.float32
     )
-    grad_act_two = lax.psum(partial_two.astype(jnp.bfloat16), "tensor").astype(jnp.float32)
+    grad_act_two = exchange_sum(partial_two)
     grad_from_two, grad_ffn_gain = pull_two(grad_act_two)
     grad_hidden = grad_out + grad_from_two
     grad_attention = grad_hidden.astype(jnp.bfloat16)
-    grad_out_w = jnp.einsum("tc,td->cd", mixed, grad_attention, preferred_element_type=jnp.float32)
+    grad_out_w = jnp.einsum("td,tc->dc", grad_attention, mixed, preferred_element_type=jnp.float32)
     grad_mixed = jnp.einsum(
         "td,cd->tc", grad_attention, w_out, preferred_element_type=jnp.float32
     ).astype(jnp.bfloat16)
@@ -208,32 +242,23 @@
     partial_one = partial_one + jnp.einsum(
         "tc,dc->td", grad_value_lin, w_value, preferred_element_type=jnp.float32
     )
-    grad_act_one = lax.psum(partial_one.astype(jnp.bfloat16), "tensor").astype(jnp.float32)
+    grad_act_one = exchange_sum(partial_one)
     grad_from_one, grad_attn_gain = pull_one(grad_act_one)
     grad_input = (grad_hidden + grad_from_one).astype(jnp.bfloat16)
-    summed = (
-        lax.psum_scatter(grad_attn_gain, "dp", scatter_dimension=0, tiled=True),
-        lax.psum_scatter(grad_query_w, "dp", scatter_dimension=0, tiled=True),
-        lax.psum_scatter(grad_key_w, "dp", scatter_dimension=0, tiled=True),
-        lax.psum_scatter(grad_value_w, "dp", scatter_dimension=0, tiled=True),
-        lax.psum_scatter(grad_out_w, "dp", scatter_dimension=1, tiled=True),
-        lax.psum_scatter(grad_ffn_gain, "dp", scatter_dimension=0, tiled=True),
-        lax.psum_scatter(grad_gate_w, "dp", scatter_dimension=0, tiled=True),
-        lax.psum_scatter(grad_up_w, "dp", scatter_dimension=0, tiled=True),
-        lax.psum_scatter(grad_down_w, "dp", scatter_dimension=1, tiled=True),
-    )
+    gains = jnp.stack([grad_attn_gain, grad_ffn_gain], axis=1)
+    gains = lax.psum_scatter(gains, "dp", scatter_dimension=0, tiled=True)
     return (
         output,
         grad_input,
-        summed[0],
-        summed[1],
-        summed[2],
-        summed[3],
-        summed[4],
-        summed[5],
-        summed[6],
-        summed[7],
-        summed[8],
+        gains[:, 0],
+        scatter_sum(grad_query_w, Y_FIRST),
+        scatter_sum(grad_key_w, X_FIRST),
+        scatter_sum(grad_value_w, X_FIRST),
+        scatter_sum(grad_out_w, X_FIRST).T,
+        gains[:, 1],
+        scatter_sum(grad_gate_w, X_FIRST),
+        scatter_sum(grad_up_w, Y_FIRST),
+        jnp.concatenate([grad_down_a.T, grad_down_b.T], axis=0),
     )
 
 

time: 1830 us -> 1020 us (0.56)
  waiting for transfers between devices: 1080 us -> 273 us
  blocking collectives: 77.4 us -> 0 us
  starting transfers between devices: 1.2 us -> 43.1 us
  local copies, waits for them, and re-layouts: 131 us -> 167 us
  matrix products: 383 us -> 357 us
  other arithmetic: 129 us -> 153 us
    reduce_scatter x7 -> x0, waiting for transfers between devices: 1040 us -> none  [the longest x1 211 us: per_device(): lax.psum_scatter(grad_down_w, 'dp', scatter_dimension=1, tiled=True)]
    ppermute x0 -> x36, waiting for transfers between devices: none -> 161 us  [the longest x32 161 us: scatter_sum(): received = lax.ppermute(sent, 'dp', pairs)]
    unnamed x10 -> x2, waiting for transfers between devices: 0.16 us -> 112 us
    unnamed x1 -> x0, blocking collectives: 77.4 us -> none
    ppermute x0 -> x36, starting transfers between devices: none -> 43.1 us  [the longest x32 42.5 us: scatter_sum(): received = lax.ppermute(sent, 'dp', pairs)]
    psum x3 -> x0, waiting for transfers between devices: 39.9 us -> none  [the longest x1 27.5 us: per_device(): lax.psum(partial_attn.astype(jnp.bfloat16), 'tensor').astype(jnp.float32)]
    convert_element_type x0 -> x24, other arithmetic: none -> 18.9 us  [scatter_sum(): work = total.astype(jnp.bfloat16) if left else total]
  transfers between devices with their start and end apart: 10 -> 37, of which waited for: 8 -> 18; matrix products, arithmetic and copies ran while one was open for 6% -> 46% of each run, Pallas kernels for 0% -> 0%
where the time goes in v1:
time: 1020 us; the launch traced here: 1010 us
  matrix products  357 us (35%)
  waiting for transfers between devices  273 us (27%)
  local copies, waits for them, and re-layouts  167 us (16%)
  other arithmetic  153 us (15%)
  starting transfers between devices  43.1 us (4%)
  between operations  15.4 us (2%)
    ppermute x32, waiting for transfers between devices, scatter_sum(): received = lax.ppermute(sent, 'dp', pairs)  161 us
    unnamed x2, waiting for transfers between devices  112 us
    dynamic_update_slice x4, local copies, waits for them, and re-layouts, per_device(): mixed, log_totals = lax.map(forward_block, (queries, allowed_blocks))  83.9 us
    dot_general x4, matrix products, block_scores(): jnp.einsum('qkgd,pkd->kgqp', query_block, keys, preferred_element_type=jn...  66.2 us
    convert_element_type x2, other arithmetic, backward_block(): grad_scores = (probs_full * (grad_probs - weighted)).astype(jnp.bfloat16)  44.4 us
    ppermute x32, starting transfers between devices, scatter_sum(): received = lax.ppermute(sent, 'dp', pairs)  42.5 us
    dot_general x2, matrix products, backward_block(): jnp.einsum('qkgd,pkd->kgqp', grad_block, values, preferred_element_type=j...  27.8 us
    reduce_sum x2, other arithmetic, forward_block(): totals = jnp.sum(shifted, axis=-1, keepdims=True)  26.8 us
  transfers between devices with their start and end apart: 37, of which 18 were waited for; matrix products, arithmetic and copies ran while one was open for 46% of the time, Pallas kernels for 0%

profile of v1, /device:TPU:0, one launch (start us, length us, event | category | flops | bytes accessed | tf_op | source)
XLA Modules:
  0.0 1009.8 jit_solution(16571398639634329150)
XLA Ops:
  42.1 84.3 %while.27 = (s32[]{:T(128)}, bf16[2,640,4,2,96]{1,4,3,2,0:T(8,128)(2,1)}, f32[2,4,2,640]{3,2,1,0:T(2,128)S(1)}, pred[2,640,1280]{2,1,0:T(8,128)(4,1)}, bf16[2,64...) while((s32[]{:T(128)}, ...), condition=%wide.region_5.6_spmd, body=%wide.region_2.5_spmd.sunk | while | flops 2595220480 | bytes 103547048 | solution.py:143
  43.7 13.0 %bitcast_reduce_fusion.2 = (f32[4,2,640]{2,1,0:T(2,128)S(1)}, f32[4,640,2,1280]{3,1,2,0:T(8,128)}) fusion(pred[640,1280]{1,0:T(8,128)(4,1)S(1)} %dynamic-slice_bitcast_fusion.31, bf16[1280,4,96]{0,2,1:T(8,128)(2,1)S(1)} %get-tuple-element.420, bf16[2,640,4,2,96]{1,4,3,2,0:T(8,128)(2,1)} %get-tuple-element.419, s32[]{:T(128)S(6)} %copy.179), kind=kOutput, calls=%fused_computation.1.clone.1 | convolution fusion | flops 1277946880 | bytes 29020164 | tf_op jit(solution)/shard_map/while/body/eval_jaxpr/qkgd,pkd->kgqp/dot_general | solution.py:51
  56.7 13.4 %fusion.169 = f32[4,2,640]{2,1,0:T(2,128)S(1)} fusion(f32[4,640,2,1280]{3,1,2,0:T(8,128)} %get-tuple-element.385, f32[4,2,640]{2,1,0:T(2,128)S(1)} %get-tuple-element.386, pred[640,1280]{1,0:T(8,128)(4,1)S(1)} %dynamic-slice_bitcast_fusion.31), kind=kLoop, calls=%fused_computation.5.clone.1 | loop fusion | flops 26209280 | bytes 27074560 | tf_op jit(solution)/shard_map/while/body/eval_jaxpr/reduce_sum | solution.py:138
  98.7 13.4 %fusion.169 = f32[4,2,640]{2,1,0:T(2,128)S(1)} fusion(f32[4,640,2,1280]{3,1,2,0:T(8,128)} %get-tuple-element.385, f32[4,2,640]{2,1,0:T(2,128)S(1)} %get-tuple-element.386, pred[640,1280]{1,0:T(8,128)(4,1)S(1)} %dynamic-slice_bitcast_fusion.31), kind=kLoop, calls=%fused_computation.5.clone.1 | loop fusion | flops 26209280 | bytes 27074560 | tf_op jit(solution)/shard_map/while/body/eval_jaxpr/reduce_sum | solution.py:138
  136.1 14.2 %fusion.114 = f32[1280,2048]{1,0:T(8,128)} fusion(bf16[1280,1536]{1,0:T(8,128)(2,1)} %param.27, bf16[2048,1536]{1,0:T(8,128)(2,1)} %param.26), kind=kOutput, calls=%fused_computation.269 | convolution fusion | flops 8053063680 | bytes 20709376 | tf_op jit(solution)/shard_map/td,fd->tf/dot_general | solution.py:165
  160.6 13.0 %fusion.113 = f32[1280,2048]{1,0:T(8,128)} fusion(bf16[1280,1536]{1,0:T(8,128)(2,1)S(1)} %multiply_convert_fusion.2, bf16[1536,2048]{1,0:T(8,128)(2,1)} %param.25), kind=kOutput, calls=%fused_computation.268 | convolution fusion | flops 8053063680 | bytes 20709376 | tf_op jit(solution)/shard_map/dot_general | solution.py:150
  173.6 23.8 %multiply_convert_fusion = (bf16[1280,2048]{1,0:T(8,128)(2,1)}, bf16[1280,2048]{1,0:T(8,128)(2,1)}, bf16[1280,2048]{1,0:T(8,128)(2,1)}) fusion(f32[1280,2048]{1,0:T(8,128)} %fusion.114, f32[1280,2048]{1,0:T(8,128)} %fusion.113, bf16[1280,1536]{1,0:T(8,128)(2,1)} %copy-done.24, bf16[1536,2048]{1,0:T(8,128)(2,1)} %param.24), kind=kOutput, calls=%fused_computation.63 | convolution fusion | flops 8095006720 | bytes 46923776 | tf_op jit(solution)/shard_map/dot_general | solution.py:149
  256.7 13.3 %fusion.55 = bf16[1280,1536]{1,0:T(8,128)(2,1)S(1)} fusion(f32[1280,1536]{1,0:T(8,128)} %fusion.115, bf16[1280,2048]{1,0:T(8,128)(2,1)} %get-tuple-element.246, bf16[1536,2048]{1,0:T(8,128)(2,1)} %param.25), kind=kOutput, calls=%fused_computation.86 | convolution fusion | flops 8056995840 | bytes 23330816 | tf_op jit(solution)/shard_map/tf,df->td/dot_general | solution.py:174
  270.0 13.1 %convolution_convert_fusion.1 = bf16[1536,2048]{1,0:T(8,128)(2,1)} fusion(bf16[1280,1536]{1,0:T(8,128)(2,1)S(1)} %copy-done.25, bf16[1280,2048]{1,0:T(8,128)(2,1)} %get-tuple-element.247), kind=kOutput, calls=%fused_computation.88 | convolution fusion | flops 8056209408 | bytes 15466496 | tf_op jit(solution)/shard_map/td,tf->df/dot_general | solution.py:169
  312.4 13.6 %convolution_convert_fusion.3 = bf16[1280,1536]{1,0:T(8,128)(2,1)} fusion(bf16[1280,2048]{1,0:T(8,128)(2,1)} %get-tuple-element.248, bf16[2048,1536]{1,0:T(8,128)(2,1)} %param.26), kind=kOutput, calls=%fused_computation.91 | convolution fusion | flops 8055029760 | bytes 15466496 | tf_op jit(solution)/shard_map/dot_general | solution.py:153
  351.4 23.8 %collective-permute-done.24 = bf16[2,2,2,96,2048]{4,3,0,1,2:T(8,128)(2,1)S(1)} collective-permute-done((bf16[2,2,2,96,2048]{4,3,0,1,2:T(8,128)(2,1)S(1)}, bf16[2,2,2,96,2048]{4,3,0,1,2:T(8,128)(2,1)S(1)}, u32[]{:S(2)}, u32[]{:S(2)}) %collective-permute-start.24) | collective-permute-done | bytes 3145760 | tf_op jit(solution)/shard_map/ppermute | solution.py:81
  434.7 260.4 %while.28 = (s32[]{:T(128)}, f32[1280,4,96]{0,2,1:T(8,128)}, f32[1280,4,96]{0,2,1:T(8,128)}, f32[2,640,4,2,96]{1,0,4,3,2:T(2,128)}, bf16[2,640,4,2,96]{1,4,3,2,0...) while((s32[]{:T(128)}, f32[1280,4,96]{0,2,1:T(8,128)}, ...), condition=%wide.region_10.11_spmd.clone, body=%wide.region_8.10_spmd.clone.sunk | while | flops 6353382400 | bytes 255201552 | solution.py:217
  436.1 13.9 %fusion.178 = f32[4,640,2,1280]{3,1,2,0:T(8,128)} fusion(bf16[1280,4,96]{0,2,1:T(8,128)(2,1)} %get-tuple-element.456, bf16[2,640,4,2,96]{1,4,3,2,0:T(8,128)(2,1)} %get-tuple-element.455, s32[]{:T(128)S(6)} %copy.189), kind=kOutput, calls=%fused_computation.35.clone.1 | convolution fusion | flops 1258291200 | bytes 28180484 | tf_op jit(solution)/shard_map/while/body/eval_jaxpr/qkgd,pkd->kgqp/dot_general | solution.py:192
  450.0 20.1 %fusion.179 = (f32[4,2,640]{2,1,0:T(2,128)S(1)}, f32[4,2,640,1280]{3,2,1,0:T(8,128)}) fusion(f32[4,640,2,1280]{3,1,2,0:T(8,128)} %fusion.178, f32[4,2,640]{2,1,0:T(2,128)S(1)} %dynamic-slice_bitcast_fusion.32, bf16[1280,4,96]{0,2,1:T(8,128)(2,1)S(1)} %get-tuple-element.453, bf16[2,640,4,2,96]{1,4,3,2,0:T(8,128)(2,1)S(1)} %copy-done.9, ...), kind=kOutput, calls=%fused_computation.20.clone.1 | convolution fusion | flops 1291054080 | bytes 55255044 | tf_op jit(solution)/shard_map/while/body/eval_jaxpr/qkgd,pkd->kgqp/dot_general | solution.py:51
  470.1 22.2 %fusion.180 = bf16[4,2,640,1280]{3,2,1,0:T(8,128)(2,1)} fusion(f32[4,2,640,1280]{3,2,1,0:T(8,128)} %get-tuple-element.397, f32[4,640,2,1280]{3,1,2,0:T(8,128)} %fusion.178, f32[4,2,640]{2,1,0:T(2,128)S(1)} %get-tuple-element.398), kind=kLoop, calls=%fused_computation.22.clone.1 | loop fusion | flops 19660800 | bytes 65556480 | tf_op jit(solution)/shard_map/while/body/eval_jaxpr/convert_element_type | solution.py:196
  526.1 38.4 %dynamic_update_slice.19 = f32[2,640,4,2,96]{1,0,4,3,2:T(2,128)} dynamic-update-slice(f32[2,640,4,2,96]{1,0,4,3,2:T(2,128)} %get-tuple-element.438, f32[1,640,4,2,96]{1,0,4,3,2:T(1,128)S(1)} %copy.172, s32[]{:T(128)S(6)} %copy.189, s32[]{:T(128)} %constant.256.clone.1..sunk, s32[]{:T(128)} %constant.256.clone.1..sunk, s32[]{:T(128)} %constant.256.clone.1..sunk, s32[]{:T(128)} %constant.256.clone.1..sunk) | dynamic-update-slice | bytes 3932164 | tf_op jit(solution)/shard_map/while/body/jit(dynamic_update_index_in_dim)/dynamic_update_slice | solution.py:143
  565.7 13.9 %fusion.178 = f32[4,640,2,1280]{3,1,2,0:T(8,128)} fusion(bf16[1280,4,96]{0,2,1:T(8,128)(2,1)} %get-tuple-element.456, bf16[2,640,4,2,96]{1,4,3,2,0:T(8,128)(2,1)} %get-tuple-element.455, s32[]{:T(128)S(6)} %copy.189), kind=kOutput, calls=%fused_computation.35.clone.1 | convolution fusion | flops 1258291200 | bytes 28180484 | tf_op jit(solution)/shard_map/while/body/eval_jaxpr/qkgd,pkd->kgqp/dot_general | solution.py:192
  579.6 20.1 %fusion.179 = (f32[4,2,640]{2,1,0:T(2,128)S(1)}, f32[4,2,640,1280]{3,2,1,0:T(8,128)}) fusion(f32[4,640,2,1280]{3,1,2,0:T(8,128)} %fusion.178, f32[4,2,640]{2,1,0:T(2,128)S(1)} %dynamic-slice_bitcast_fusion.32, bf16[1280,4,96]{0,2,1:T(8,128)(2,1)S(1)} %get-tuple-element.453, bf16[2,640,4,2,96]{1,4,3,2,0:T(8,128)(2,1)S(1)} %copy-done.9, ...), kind=kOutput, calls=%fused_computation.20.clone.1 | convolution fusion | flops 1291054080 | bytes 55255044 | tf_op jit(solution)/shard_map/while/body/eval_jaxpr/qkgd,pkd->kgqp/dot_general | solution.py:51
  599.7 22.2 %fusion.180 = bf16[4,2,640,1280]{3,2,1,0:T(8,128)(2,1)} fusion(f32[4,2,640,1280]{3,2,1,0:T(8,128)} %get-tuple-element.397, f32[4,640,2,1280]{3,1,2,0:T(8,128)} %fusion.178, f32[4,2,640]{2,1,0:T(2,128)S(1)} %get-tuple-element.398), kind=kLoop, calls=%fused_computation.22.clone.1 | loop fusion | flops 19660800 | bytes 65556480 | tf_op jit(solution)/shard_map/while/body/eval_jaxpr/convert_element_type | solution.py:196
  656.3 38.4 %dynamic_update_slice.19 = f32[2,640,4,2,96]{1,0,4,3,2:T(2,128)} dynamic-update-slice(f32[2,640,4,2,96]{1,0,4,3,2:T(2,128)} %get-tuple-element.438, f32[1,640,4,2,96]{1,0,4,3,2:T(1,128)S(1)} %copy.172, s32[]{:T(128)S(6)} %copy.189, s32[]{:T(128)} %constant.256.clone.1..sunk, s32[]{:T(128)} %constant.256.clone.1..sunk, s32[]{:T(128)} %constant.256.clone.1..sunk, s32[]{:T(128)} %constant.256.clone.1..sunk) | dynamic-update-slice | bytes 3932164 | tf_op jit(solution)/shard_map/while/body/jit(dynamic_update_index_in_dim)/dynamic_update_slice | solution.py:143
  729.7 24.2 %collective-permute-done.8 = bf16[2,2,2,96,384]{4,3,0,1,2:T(8,128)(2,1)S(1)} collective-permute-done((bf16[2,2,2,96,384]{4,3,0,1,2:T(8,128)(2,1)}, bf16[2,2,2,96,384]{4,3,0,1,2:T(8,128)(2,1)S(1)}, u32[]{:S(2)}, u32[]{:S(2)}) %collective-permute-start.8) | collective-permute-done | bytes 589856 | tf_op jit(solution)/shard_map/ppermute | solution.py:81
  770.3 15.4 %collective-permute-done.9 = bf16[2,2,96,384]{3,2,0,1:T(8,128)(2,1)S(1)} collective-permute-done((bf16[2,2,96,384]{3,2,0,1:T(8,128)(2,1)S(1)}, bf16[2,2,96,384]{3,2,0,1:T(8,128)(2,1)S(1)}, u32[]{:S(2)}, u32[]{:S(2)}) %collective-permute-start.9) | collective-permute-done | bytes 294944 | tf_op jit(solution)/shard_map/ppermute | solution.py:81
  832.2 17.1 %collective-permute-done.22 = bf16[2,96,2048]{2,1,0:T(8,128)(2,1)S(1)} collective-permute-done((bf16[2,96,2048]{2,1,0:T(8,128)(2,1)S(1)}, bf16[2,96,2048]{2,1,0:T(8,128)(2,1)S(1)}, u32[]{:S(2)}, u32[]{:S(2)}) %collective-permute-start.22) | collective-permute-done | bytes 786464 | tf_op jit(solution)/shard_map/ppermute | solution.py:81
  888.6 112.1 %reduce-scatter.4.cloned.1.call-done = f32[96,2]{1,0:T(8,128)} async-done(((f32[1536,2]{1,0:T(8,128)}), f32[96,2]{1,0:T(8,128)}) %reduce-scatter.4.cloned.1.call-update) | async-done | bytes 784
  (368 shorter events, 480.6 us)
Async XLA Ops:
  7.2 993.4 %reduce-scatter.4.cloned.1.call-start = ((), (), s32[]{:S(2)}) async-start(), calls=%async_computation.1 | async-start | bytes 835584
  221.5 61.6 %collective-permute-start.32 = (bf16[2,2,2,96,1024]{4,3,0,1,2:T(8,128)(2,1)}, bf16[2,2,2,96,1024]{4,3,0,1,2:T(8,128)(2,1)}, u32[]{:S(2)}, u32[]{:S(2)}) collective-permute-start(bf16[2,2,2,96,1024]{4,3,0,1,2:T(8,128)(2,1)} %bitcast.357), channel_id=1, source_target_pairs={{0,4},{2,6},{4,0},{6,2},{8,12},{10,14},{12,8},{14,10},{16,20},{18,... | collective-permute-start | bytes 4718600 | tf_op jit(solution)/shard_map/ppermute | solution.py:81
  230.8 56.1 %collective-permute-start.28 = (bf16[2,2,2,96,1024]{4,3,2,1,0:T(8,128)(2,1)S(1)}, bf16[2,2,2,96,1024]{4,3,2,1,0:T(8,128)(2,1)S(1)}, u32[]{:S(2)}, u32[]{:S(2)}) collective-permute-start(bf16[2,2,2,96,1024]{4,3,2,1,0:T(8,128)(2,1)S(1)} %dynamic-slice_bitcast_fusion.3), channel_id=1, source_target_pairs={{0,2},{2,0},{4,6},{6,4},{8,10},{10,8},{12,14},{14,12},{16,18},{18,... | collective-permute-start | bytes 4718600 | tf_op jit(solution)/shard_map/ppermute | solution.py:81
  286.3 20.7 %collective-permute-start.33 = (bf16[2,2,96,1024]{3,2,0,1:T(8,128)(2,1)}, bf16[2,2,96,1024]{3,2,0,1:T(8,128)(2,1)}, u32[]{:S(2)}, u32[]{:S(2)}) collective-permute-start(bf16[2,2,96,1024]{3,2,0,1:T(8,128)(2,1)} %dynamic-slice_bitcast_fusion.6), channel_id=1, source_target_pairs={{0,2},{2,0},{4,6},{6,4},{8,10},{10,8},{12,14},{14,12},{16,18},{18,... | collective-permute-start | bytes 2359304 | tf_op jit(solution)/shard_map/ppermute | solution.py:81
  288.5 21.7 %collective-permute-start.29 = (bf16[2,2,96,1024]{3,2,1,0:T(8,128)(2,1)}, bf16[2,2,96,1024]{3,2,1,0:T(8,128)(2,1)}, u32[]{:S(2)}, u32[]{:S(2)}) collective-permute-start(bf16[2,2,96,1024]{3,2,1,0:T(8,128)(2,1)} %dynamic-slice_bitcast_fusion.7), channel_id=1, source_target_pairs={{0,4},{2,6},{4,0},{6,2},{8,12},{10,14},{12,8},{14,10},{16,20},{18,... | collective-permute-start | bytes 2359304 | tf_op jit(solution)/shard_map/ppermute | solution.py:81
  295.2 80.0 %collective-permute-start.24 = (bf16[2,2,2,96,2048]{4,3,0,1,2:T(8,128)(2,1)S(1)}, bf16[2,2,2,96,2048]{4,3,0,1,2:T(8,128)(2,1)S(1)}, u32[]{:S(2)}, u32[]{:S(2)}) collective-permute-start(bf16[2,2,2,96,2048]{4,3,0,1,2:T(8,128)(2,1)S(1)} %bitcast.427), channel_id=1, source_target_pairs={{0,4},{2,6},{4,0},{6,2},{8,12},{10,14},{12,8},{14,10},{16,20},{18,... | collective-permute-start | bytes 9437192 | tf_op jit(solution)/shard_map/ppermute | solution.py:81
  297.3 87.4 %collective-permute-start.20 = (bf16[2,2,2,96,2048]{4,3,0,1,2:T(8,128)(2,1)}, bf16[2,2,2,96,2048]{4,3,0,1,2:T(8,128)(2,1)S(1)}, u32[]{:S(2)}, u32[]{:S(2)}) collective-permute-start(bf16[2,2,2,96,2048]{4,3,0,1,2:T(8,128)(2,1)} %bitcast.356), channel_id=1, source_target_pairs={{0,2},{2,0},{4,6},{6,4},{8,10},{10,8},{12,14},{14,12},{16,18},{18,... | collective-permute-start | bytes 9437192 | tf_op jit(solution)/shard_map/ppermute | solution.py:81
  298.8 92.7 %collective-permute-start.2 = (bf16[1280,1536]{1,0:T(8,128)(2,1)S(1)}, bf16[1280,1536]{1,0:T(8,128)(2,1)S(1)}, u32[]{:S(2)}, u32[]{:S(2)}) collective-permute-start(bf16[1280,1536]{1,0:T(8,128)(2,1)S(1)} %fusion.55), channel_id=1, source_target_pairs={{0,1},{1,0},{2,3},{3,2},{4,5},{5,4},{6,7},{7,6},{8,9},{9,8},{10,11... | collective-permute-start | bytes 11796488 | tf_op jit(solution)/shard_map/ppermute | solution.py:63
  308.6 17.5 %collective-permute-start.34 = (bf16[2,96,1024]{2,1,0:T(8,128)(2,1)S(1)}, bf16[2,96,1024]{2,1,0:T(8,128)(2,1)S(1)}, u32[]{:S(2)}, u32[]{:S(2)}) collective-permute-start(bf16[2,96,1024]{2,1,0:T(8,128)(2,1)S(1)} %dynamic-slice_bitcast_fusion.12), channel_id=1, source_target_pairs={{0,8},{2,10},{4,12},{6,14},{8,0},{10,2},{12,4},{14,6},{16,24},{18,... | collective-permute-start | bytes 1179656 | tf_op jit(solution)/shard_map/ppermute | solution.py:81
  326.1 69.3 %collective-permute-start.1 = (bf16[1280,1536]{1,0:T(8,128)(2,1)}, bf16[1280,1536]{1,0:T(8,128)(2,1)}, u32[]{:S(2)}, u32[]{:S(2)}) collective-permute-start(bf16[1280,1536]{1,0:T(8,128)(2,1)} %convolution_convert_fusion.3), channel_id=1, source_target_pairs={{0,1},{1,0},{2,3},{3,2},{4,5},{5,4},{6,7},{7,6},{8,9},{9,8},{10,11... | collective-permute-start | bytes 11796488 | tf_op jit(solution)/shard_map/ppermute | solution.py:63
  383.2 380.8 %collective-permute-start.25 = (bf16[2,2,96,2048]{3,2,0,1:T(8,128)(2,1)}, bf16[2,2,96,2048]{3,2,0,1:T(8,128)(2,1)}, u32[]{:S(2)}, u32[]{:S(2)}) collective-permute-start(bf16[2,2,96,2048]{3,2,0,1:T(8,128)(2,1)} %dynamic-slice_bitcast_fusion.4), channel_id=1, source_target_pairs={{0,2},{2,0},{4,6},{6,4},{8,10},{10,8},{12,14},{14,12},{16,18},{18,... | collective-permute-start | bytes 4718600 | tf_op jit(solution)/shard_map/ppermute | solution.py:81
  391.0 376.6 %collective-permute-start.21 = (bf16[2,2,96,2048]{3,2,0,1:T(8,128)(2,1)}, bf16[2,2,96,2048]{3,2,0,1:T(8,128)(2,1)}, u32[]{:S(2)}, u32[]{:S(2)}) collective-permute-start(bf16[2,2,96,2048]{3,2,0,1:T(8,128)(2,1)} %dynamic-slice_bitcast_fusion.5), channel_id=1, source_target_pairs={{0,4},{2,6},{4,0},{6,2},{8,12},{10,14},{12,8},{14,10},{16,20},{18,... | collective-permute-start | bytes 4718600 | tf_op jit(solution)/shard_map/ppermute | solution.py:81
  712.4 112.0 %collective-permute-start.16 = (bf16[2,2,2,96,768]{4,3,0,1,2:T(8,128)(2,1)S(1)}, bf16[2,2,2,96,768]{4,3,0,1,2:T(8,128)(2,1)S(1)}, u32[]{:S(2)}, u32[]{:S(2)}) collective-permute-start(bf16[2,2,2,96,768]{4,3,0,1,2:T(8,128)(2,1)S(1)} %bitcast.437), channel_id=1, source_target_pairs={{0,2},{2,0},{4,6},{6,4},{8,10},{10,8},{12,14},{14,12},{16,18},{18,... | collective-permute-start | bytes 3538952 | tf_op jit(solution)/shard_map/ppermute | solution.py:81
  722.5 31.5 %collective-permute-start.8 = (bf16[2,2,2,96,384]{4,3,0,1,2:T(8,128)(2,1)}, bf16[2,2,2,96,384]{4,3,0,1,2:T(8,128)(2,1)S(1)}, u32[]{:S(2)}, u32[]{:S(2)}) collective-permute-start(bf16[2,2,2,96,384]{4,3,0,1,2:T(8,128)(2,1)} %bitcast.361), channel_id=1, source_target_pairs={{0,2},{2,0},{4,6},{6,4},{8,10},{10,8},{12,14},{14,12},{16,18},{18,... | collective-permute-start | bytes 1769480 | tf_op jit(solution)/shard_map/ppermute | solution.py:81
  723.9 39.8 %collective-permute-start.12 = (bf16[2,2,2,96,384]{4,3,0,1,2:T(8,128)(2,1)}, bf16[2,2,2,96,384]{4,3,0,1,2:T(8,128)(2,1)S(1)}, u32[]{:S(2)}, u32[]{:S(2)}) collective-permute-start(bf16[2,2,2,96,384]{4,3,0,1,2:T(8,128)(2,1)} %bitcast.360), channel_id=1, source_target_pairs={{0,2},{2,0},{4,6},{6,4},{8,10},{10,8},{12,14},{14,12},{16,18},{18,... | collective-permute-start | bytes 1769480 | tf_op jit(solution)/shard_map/ppermute | solution.py:81
  754.0 72.0 %collective-permute-start.4 = (bf16[2,2,2,96,768]{4,3,0,1,2:T(8,128)(2,1)S(1)}, bf16[2,2,2,96,768]{4,3,0,1,2:T(8,128)(2,1)S(1)}, u32[]{:S(2)}, u32[]{:S(2)}) collective-permute-start(bf16[2,2,2,96,768]{4,3,0,1,2:T(8,128)(2,1)S(1)} %bitcast.438), channel_id=1, source_target_pairs={{0,4},{2,6},{4,0},{6,2},{8,12},{10,14},{12,8},{14,10},{16,20},{18,... | collective-permute-start | bytes 3538952 | tf_op jit(solution)/shard_map/ppermute | solution.py:81
  763.8 109.9 %collective-permute-start.3 = (bf16[1280,1536]{1,0:T(8,128)(2,1)S(1)}, bf16[1280,1536]{1,0:T(8,128)(2,1)S(1)}, u32[]{:S(2)}, u32[]{:S(2)}) collective-permute-start(bf16[1280,1536]{1,0:T(8,128)(2,1)S(1)} %fusion.56), channel_id=1, source_target_pairs={{0,1},{1,0},{2,3},{3,2},{4,5},{5,4},{6,7},{7,6},{8,9},{9,8},{10,11... | collective-permute-start | bytes 11796488 | tf_op jit(solution)/shard_map/ppermute | solution.py:63
  764.0 21.8 %collective-permute-start.9 = (bf16[2,2,96,384]{3,2,0,1:T(8,128)(2,1)S(1)}, bf16[2,2,96,384]{3,2,0,1:T(8,128)(2,1)S(1)}, u32[]{:S(2)}, u32[]{:S(2)}) collective-permute-start(bf16[2,2,96,384]{3,2,0,1:T(8,128)(2,1)S(1)} %dynamic-slice_bitcast_fusion.18), channel_id=1, source_target_pairs={{0,4},{2,6},{4,0},{6,2},{8,12},{10,14},{12,8},{14,10},{16,20},{18,... | collective-permute-start | bytes 884744 | tf_op jit(solution)/shard_map/ppermute | solution.py:81
  767.6 21.3 %collective-permute-start.13 = (bf16[2,2,96,384]{3,2,0,1:T(8,128)(2,1)S(1)}, bf16[2,2,96,384]{3,2,0,1:T(8,128)(2,1)S(1)}, u32[]{:S(2)}, u32[]{:S(2)}) collective-permute-start(bf16[2,2,96,384]{3,2,0,1:T(8,128)(2,1)S(1)} %dynamic-slice_bitcast_fusion.17), channel_id=1, source_target_pairs={{0,4},{2,6},{4,0},{6,2},{8,12},{10,14},{12,8},{14,10},{16,20},{18,... | collective-permute-start | bytes 884744 | tf_op jit(solution)/shard_map/ppermute | solution.py:81
  785.7 41.6 %collective-permute-start.26 = (bf16[2,96,2048]{2,1,0:T(8,128)(2,1)S(1)}, bf16[2,96,2048]{2,1,0:T(8,128)(2,1)S(1)}, u32[]{:S(2)}, u32[]{:S(2)}) collective-permute-start(bf16[2,96,2048]{2,1,0:T(8,128)(2,1)S(1)} %dynamic-slice_bitcast_fusion.8), channel_id=1, source_target_pairs={{0,8},{2,10},{4,12},{6,14},{8,0},{10,2},{12,4},{14,6},{16,24},{18,... | collective-permute-start | bytes 2359304 | tf_op jit(solution)/shard_map/ppermute | solution.py:81
  823.7 25.6 %collective-permute-start.22 = (bf16[2,96,2048]{2,1,0:T(8,128)(2,1)S(1)}, bf16[2,96,2048]{2,1,0:T(8,128)(2,1)S(1)}, u32[]{:S(2)}, u32[]{:S(2)}) collective-permute-start(bf16[2,96,2048]{2,1,0:T(8,128)(2,1)S(1)} %dynamic-slice_bitcast_fusion.9), channel_id=1, source_target_pairs={{0,8},{2,10},{4,12},{6,14},{8,0},{10,2},{12,4},{14,6},{16,24},{18,... | collective-permute-start | bytes 2359304 | tf_op jit(solution)/shard_map/ppermute | solution.py:81
  824.8 25.2 %collective-permute-start.17 = (bf16[2,2,96,768]{3,2,0,1:T(8,128)(2,1)S(1)}, bf16[2,2,96,768]{3,2,0,1:T(8,128)(2,1)S(1)}, u32[]{:S(2)}, u32[]{:S(2)}) collective-permute-start(bf16[2,2,96,768]{3,2,0,1:T(8,128)(2,1)S(1)} %dynamic-slice_bitcast_fusion.10), channel_id=1, source_target_pairs={{0,4},{2,6},{4,0},{6,2},{8,12},{10,14},{12,8},{14,10},{16,20},{18,... | collective-permute-start | bytes 1769480 | tf_op jit(solution)/shard_map/ppermute | solution.py:81
  826.4 26.4 %collective-permute-start.5 = (bf16[2,2,96,768]{3,2,0,1:T(8,128)(2,1)S(1)}, bf16[2,2,96,768]{3,2,0,1:T(8,128)(2,1)S(1)}, u32[]{:S(2)}, u32[]{:S(2)}) collective-permute-start(bf16[2,2,96,768]{3,2,0,1:T(8,128)(2,1)S(1)} %dynamic-slice_bitcast_fusion.11), channel_id=1, source_target_pairs={{0,2},{2,0},{4,6},{6,4},{8,10},{10,8},{12,14},{14,12},{16,18},{18,... | collective-permute-start | bytes 1769480 | tf_op jit(solution)/shard_map/ppermute | solution.py:81
  827.7 25.4 %collective-permute-start.27 = (bf16[96,2048]{1,0:T(8,128)(2,1)S(1)}, bf16[96,2048]{1,0:T(8,128)(2,1)S(1)}, u32[]{:S(2)}, u32[]{:S(2)}) collective-permute-start(bf16[96,2048]{1,0:T(8,128)(2,1)S(1)} %dynamic-slice_bitcast_fusion.14), channel_id=1, source_target_pairs={{0,16},{2,18},{4,20},{6,22},{8,24},{10,26},{12,28},{14,30},{16,0},... | collective-permute-start | bytes 1179656 | tf_op jit(solution)/shard_map/ppermute | solution.py:81
  (81 other events, 1048.9 us)
Sparse Core Ops, SparseCore 0:
  878.5 122.0 reduce-scatter.3

commit v2 on v1

v2 whole, which is shorter than its diff:
```python
import jax
import jax.numpy as jnp
import numpy as np
from jax import lax
from jax.experimental import pallas as pl
from jax.experimental.pallas import tpu as pltpu
from jax.sharding import PartitionSpec as P

HEAD_DIM = 96
PROMPT = 1024
CONT_LEN = 128
CONT = 2
GROUP_TOK = 1280
BLOCK = 256
BLOCKS = GROUP_TOK // BLOCK
LANES = 128
MIB = 1 << 20
epsilon = 1e-05
rope_base = 100000.0
LOG2E = 1.4426950408889634
SCORE_SCALE = HEAD_DIM ** (-0.5)
NT = (((1,), (1,)), ((), ()))
TN = (((0,), (0,)), ((), ()))


def matmul(left, right, dims=(((1,), (0,)), ((), ()))):
    return lax.dot_general(left, right, dims, preferred_element_type=jnp.float32)


def rope_tables(branch):
    half = HEAD_DIM // 2
    frequency = rope_base ** (-np.arange(half, dtype=np.float64) * 2.0 / HEAD_DIM)
    angles = np.arange(PROMPT + CONT_LEN, dtype=np.float64)[:, None] * frequency[None, :]
    pad = np.zeros((angles.shape[0], LANES - HEAD_DIM))
    cosine = np.concatenate([np.cos(angles), np.cos(angles), pad], axis=1)
    sine = np.concatenate([-np.sin(angles), np.sin(angles), pad], axis=1)
    both = jnp.asarray(np.stack([cosine, sine]), jnp.float32)
    parts = [both[:, :PROMPT]]
    for c in range(CONT):
        parts.append(lax.dynamic_slice_in_dim(both, branch[c], CONT_LEN, axis=1))
    return jnp.concatenate(parts, axis=1)


def lane_ids(shape):
    return lax.broadcasted_iota(jnp.int32, shape, 1)


def swap_halves(head):
    half = HEAD_DIM // 2
    return jnp.where(
        lane_ids(head.shape) < half, pltpu.roll(head, LANES - half, 1), pltpu.roll(head, half, 1)
    )


def take_head(full, h):
    first = h * HEAD_DIM
    start, shift = first // LANES * LANES, first % LANES
    width = LANES if shift + HEAD_DIM <= LANES else 2 * LANES
    part = full[:, start : start + width]
    return part[:, :LANES] if shift == 0 else pltpu.roll(part, width - shift, 1)[:, :LANES]


def join_heads(heads):
    lanes = lane_ids(heads[0].shape)
    out = []
    for i in range(0, len(heads), 4):
        one, two, three = (pltpu.roll(heads[i + j], LANES - 32 * j, 1) for j in (1, 2, 3))
        out.append(jnp.where(lanes < 96, heads[i], one))
        out.append(jnp.where(lanes < 64, one, two))
        out.append(jnp.where(lanes < 32, two, three))
    return jnp.concatenate(out, axis=1)


def own_mask(shape, query_axis, block):
    query = lax.broadcasted_iota(jnp.int32, shape, query_axis) & (BLOCK - 1)
    key = lax.broadcasted_iota(jnp.int32, shape, 1 - query_axis)
    mask = key <= query
    if block * BLOCK >= PROMPT:
        mask = mask & ((key // CONT_LEN) == (query // CONT_LEN))
    return mask


def reach_mask(shape, query_axis, branch_ref):
    query = lax.broadcasted_iota(jnp.int32, shape, query_axis) & (BLOCK - 1)
    key = lax.broadcasted_iota(jnp.int32, shape, 1 - query_axis) + PROMPT // 2
    return key < jnp.where(query < CONT_LEN, branch_ref[0, 0], branch_ref[0, 1])


def attention_forward_kernel(
    branch_ref, x_ref, gain_ref, wq_ref, wk_ref, wv_ref, wo_ref, rope_ref,
    act_ref, q_ref, k_ref, v_ref, mixed_ref, lse_ref, part_ref, o_ref,
):
    kv_heads = k_ref.shape[0]
    group = 2 * BLOCK

    def project(i, carry):
        rows = pl.ds(pl.multiple_of(i * BLOCK, BLOCK), BLOCK)
        x = x_ref[rows, :].astype(jnp.float32)
        norm = lax.rsqrt(jnp.mean(x * x, axis=-1, keepdims=True) + epsilon)
        act = (x * norm * gain_ref[...]).astype(jnp.bfloat16)
        act_ref[rows, :] = act
        cosine, sine = rope_ref[0, rows, :], rope_ref[1, rows, :]
        full = matmul(act, wq_ref[...])
        for h in range(2 * kv_heads):
            head = take_head(full, h)
            rotated = head * cosine + swap_halves(head) * sine
            q_ref[h // 2, i, pl.ds(h % 2 * BLOCK, BLOCK), :] = rotated.astype(jnp.bfloat16)
        full = matmul(act, wk_ref[...])
        for h in range(kv_heads):
            head = take_head(full, h)
            rotated = head * cosine + swap_halves(head) * sine
            k_ref[h, rows, :] = rotated.astype(jnp.bfloat16)
        full = matmul(act, wv_ref[...])
        lanes = lane_ids((BLOCK, LANES))
        for h in range(kv_heads):
            head = jnp.where(lanes < HEAD_DIM, take_head(full, h), 0.0)
            v_ref[h, rows, :] = jnp.where(lanes == HEAD_DIM, 1.0, head).astype(jnp.bfloat16)
        return carry

    lax.fori_loop(0, BLOCKS, project, 0)

    factor = SCORE_SCALE * LOG2E

    def attend(h, carry):
        for i in range(BLOCKS):
            query = q_ref[h, i]
            before = i * BLOCK
            own = matmul(query, k_ref[h, before : before + BLOCK], NT)
            own = jnp.where(own_mask(own.shape, 0, i), own, -1e30)
            largest = jnp.max(own, axis=-1, keepdims=True)
            spans = []
            if i > 0:
                cuts = [0, before] if before < PROMPT else [0, PROMPT // 2, PROMPT]
                for low, high in zip(cuts[:-1], cuts[1:]):
                    scores = matmul(query, k_ref[h, low:high], NT)
                    if before >= PROMPT and low > 0:
                        scores = jnp.where(reach_mask(scores.shape, 0, branch_ref), scores, -1e30)
                    largest = jnp.maximum(largest, jnp.max(scores, axis=-1, keepdims=True))
                    spans.append((low, high, scores))
            shift = largest * factor
            probs = jnp.exp2(own * factor - shift).astype(jnp.bfloat16)
            total = matmul(probs, v_ref[h, before : before + BLOCK])
            for low, high, scores in spans:
                probs = jnp.exp2(scores * factor - shift).astype(jnp.bfloat16)
                total += matmul(probs, v_ref[h, low:high])
            sums = total[:, HEAD_DIM : HEAD_DIM + 1]
            mixed = total / sums
            for g in range(2):
                o_ref[2 * h + g, before : before + BLOCK, :] = mixed[g * BLOCK : (g + 1) * BLOCK]
            logs = shift + jnp.log2(sums)
            lse_ref[h, i] = jnp.broadcast_to(logs, (group, LANES)).T[0:1, :]
        return carry

    lax.fori_loop(0, kv_heads, attend, 0)

    def finish(i, carry):
        rows = pl.ds(pl.multiple_of(i * BLOCK, BLOCK), BLOCK)
        mixed = join_heads([o_ref[h, rows, :] for h in range(2 * kv_heads)]).astype(jnp.bfloat16)
        mixed_ref[rows, :] = mixed
        part_ref[rows, :] = matmul(mixed, wo_ref[...]).astype(jnp.bfloat16)
        return carry

    lax.fori_loop(0, BLOCKS, finish, 0)


def attention_forward(branch, x, gain, wq, wk, wv, wo, rope):
    kv_heads = wk.shape[1] // HEAD_DIM
    rows, width = x.shape
    bf = jnp.bfloat16
    vmem = pl.BlockSpec(memory_space=pltpu.VMEM)
    return pl.pallas_call(
        attention_forward_kernel,
        out_shape=(
            jax.ShapeDtypeStruct((rows, width), bf),
            jax.ShapeDtypeStruct((kv_heads, BLOCKS, 2 * BLOCK, LANES), bf),
            jax.ShapeDtypeStruct((kv_heads, rows, LANES), bf),
            jax.ShapeDtypeStruct((kv_heads, rows, LANES), bf),
            jax.ShapeDtypeStruct((rows, wq.shape[1]), bf),
            jax.ShapeDtypeStruct((kv_heads, BLOCKS, 1, 2 * BLOCK), jnp.float32),
            jax.ShapeDtypeStruct((rows, width), bf),
        ),
        in_specs=[pl.BlockSpec(memory_space=pltpu.SMEM)] + [vmem] * 7,
        out_specs=[vmem] * 7,
        scratch_shapes=[pltpu.VMEM((2 * kv_heads, rows, LANES), jnp.float32)],
        compiler_params=pltpu.CompilerParams(vmem_limit_bytes=60 * MIB),
        cost_estimate=pl.CostEstimate(flops=20 * 10**9, bytes_accessed=40 * 10**6, transcendentals=0),
        name="attention_forward",
    )(branch, x, gain.reshape(1, width), wq, wk, wv, wo, rope)


def attention_backward_kernel(
    branch_ref, gatt_ref, q_ref, k_ref, v_ref, lse_ref, wo_ref, wq_ref, wk_ref, wv_ref, rope_ref,
    gq_ref, gk_ref, gv_ref, part_ref, do_ref, dq_ref, dk_ref, dv_ref,
):
    kv_heads = k_ref.shape[0]
    group = 2 * BLOCK
    factor = SCORE_SCALE * LOG2E

    def project(i, carry):
        rows = pl.ds(pl.multiple_of(i * BLOCK, BLOCK), BLOCK)
        full = matmul(gatt_ref[rows, :], wo_ref[...], NT)
        lanes = lane_ids((BLOCK, LANES))
        for h in range(2 * kv_heads):
            head = jnp.where(lanes < HEAD_DIM, take_head(full, h), 0.0)
            do_ref[h // 2, i, pl.ds(h % 2 * BLOCK, BLOCK), :] = head.astype(jnp.bfloat16)
        return carry

    lax.fori_loop(0, BLOCKS, project, 0)

    def attend(h, carry):
        for i in reversed(range(BLOCKS)):
            query, grad, logs = q_ref[h, i], do_ref[h, i], lse_ref[h, i]
            before = i * BLOCK
            cuts = [(before, before + BLOCK)]
            if i > 0 and before < PROMPT:
                cuts += [(0, before)]
            elif i > 0:
                cuts += [(0, PROMPT // 2), (PROMPT // 2, PROMPT)]
            spans, weighted = [], 0.0
            for low, high in cuts:
                scores = matmul(k_ref[h, low:high], query, NT)
                probs = jnp.exp2(scores * factor - logs)
                if low == before:
                    probs = jnp.where(own_mask(probs.shape, 1, i), probs, 0.0)
                elif before >= PROMPT and low > 0:
                    probs = jnp.where(reach_mask(probs.shape, 1, branch_ref), probs, 0.0)
                grad_probs = matmul(v_ref[h, low:high], grad, NT)
                weighted += jnp.sum(probs * grad_probs, axis=0, keepdims=True)
                spans.append((low, high, probs, grad_probs))
            grad_query = jnp.zeros((group, LANES), jnp.float32)
            for low, high, probs, grad_probs in spans:
                grad_scores = (probs * (grad_probs - weighted)).astype(jnp.bfloat16)
                grad_query += matmul(grad_scores, k_ref[h, low:high], TN)
                grad_key = matmul(grad_scores, query)
                grad_value = matmul(probs.astype(jnp.bfloat16), grad)
                if before >= PROMPT:
                    dk_ref[h, low:high] = grad_key
                    dv_ref[h, low:high] = grad_value
                else:
                    dk_ref[h, low:high] += grad_key
                    dv_ref[h, low:high] += grad_value
            dq_ref[h, i] = grad_query
        return carry

    lax.fori_loop(0, kv_heads, attend, 0)

    def finish(i, carry):
        rows = pl.ds(pl.multiple_of(i * BLOCK, BLOCK), BLOCK)
        cosine, sine = rope_ref[0, rows, :] * SCORE_SCALE, rope_ref[1, rows, :] * SCORE_SCALE
        heads = []
        for h in range(2 * kv_heads):
            head = dq_ref[h // 2, i, pl.ds(h % 2 * BLOCK, BLOCK), :]
            heads.append(head * cosine - swap_halves(head) * sine)
        grad_q = join_heads(heads).astype(jnp.bfloat16)
        heads = []
        for h in range(kv_heads):
            head = dk_ref[h, rows, :]
            heads.append(head * cosine - swap_halves(head) * sine)
        grad_k = join_heads(heads).astype(jnp.bfloat16)
        grad_v = join_heads([dv_ref[h, rows, :] for h in range(kv_heads)]).astype(jnp.bfloat16)
        gq_ref[rows, :] = grad_q
        gk_ref[rows, :] = grad_k
        gv_ref[rows, :] = grad_v
        part = matmul(grad_q, wq_ref[...], NT)
        part += matmul(grad_k, wk_ref[...], NT)
        part += matmul(grad_v, wv_ref[...], NT)
        part_ref[rows, :] = part.astype(jnp.bfloat16)
        return carry

    lax.fori_loop(0, BLOCKS, finish, 0)


def attention_backward(branch, gatt, q, k, v, lse, wo, wq, wk, wv, rope):
    kv_heads = k.shape[0]
    rows, width = gatt.shape
    bf = jnp.bfloat16
    vmem = pl.BlockSpec(memory_space=pltpu.VMEM)
    return pl.pallas_call(
        attention_backward_kernel,
        out_shape=(
            jax.ShapeDtypeStruct((rows, wq.shape[1]), bf),
            jax.ShapeDtypeStruct((rows, wk.shape[1]), bf),
            jax.ShapeDtypeStruct((rows, wv.shape[1]), bf),
            jax.ShapeDtypeStruct((rows, width), bf),
        ),
        in_specs=[pl.BlockSpec(memory_space=pltpu.SMEM)] + [vmem] * 10,
        out_specs=[vmem] * 4,
        scratch_shapes=[
            pltpu.VMEM((kv_heads, BLOCKS, 2 * BLOCK, LANES), bf),
            pltpu.VMEM((kv_heads, BLOCKS, 2 * BLOCK, LANES), jnp.float32),
            pltpu.VMEM((kv_heads, rows, LANES), jnp.float32),
            pltpu.VMEM((kv_heads, rows, LANES), jnp.float32),
        ],
        compiler_params=pltpu.CompilerParams(vmem_limit_bytes=60 * MIB),
        cost_estimate=pl.CostEstimate(flops=35 * 10**9, bytes_accessed=40 * 10**6, transcendentals=0),
        name="attention_backward",
    )(branch, gatt, q, k, v, lse, wo, wq, wk, wv, rope)


def rms_norm(values, scale_gain):
    return (
        values * lax.rsqrt(jnp.mean(values * values, axis=-1, keepdims=True) + epsilon) * scale_gain
    )


def swiglu(gate, up_proj):
    return jax.nn.silu(gate) * up_proj


def exchange_sum(partial):
    sent = partial.astype(jnp.bfloat16)
    received = lax.ppermute(sent, "tensor", [(0, 1), (1, 0)])
    return sent.astype(jnp.float32) + received.astype(jnp.float32)


def scatter_sum(grads, order):
    size = lax.axis_size("dp")
    bits = size.bit_length() - 1
    me = lax.axis_index("dp")
    work = grads.astype(jnp.bfloat16)
    rows, width = work.shape
    work = work.reshape((2,) * bits + (rows // size, width))
    left = list(range(bits))[::-1]
    for bit in [b for b in order if b < bits] + list(range(len(order), bits)):
        axis = left.index(bit)
        mine = (me >> bit) & 1
        sent = lax.dynamic_index_in_dim(work, 1 - mine, axis, keepdims=False)
        kept = lax.dynamic_index_in_dim(work, mine, axis, keepdims=False)
        pairs = [(i, i ^ (1 << bit)) for i in range(size)]
        received = lax.ppermute(sent, "dp", pairs)
        total = kept.astype(jnp.float32) + received.astype(jnp.float32)
        left.pop(axis)
        work = total.astype(jnp.bfloat16) if left else total
    return work


X_FIRST = (0, 1, 2, 3)
Y_FIRST = (1, 0, 2, 3)


def per_device(
    layer_input,
    branch_point,
    attn_gain,
    w_query,
    w_key,
    w_value,
    w_out,
    ffn_gain,
    w_gate,
    w_up,
    w_down,
    cotangent,
):
    rope = rope_tables(branch_point[0])
    inputs = layer_input.astype(jnp.float32)
    grad_out = cotangent.astype(jnp.float32)
    _, pull_one = jax.vjp(rms_norm, inputs, attn_gain)
    act_one, queries, keys, values, mixed, log_sums, partial_attn = attention_forward(
        branch_point, layer_input, attn_gain, w_query, w_key, w_value, w_out, rope
    )
    hidden_state = inputs + exchange_sum(partial_attn)
    normed_two, pull_two = jax.vjp(rms_norm, hidden_state, ffn_gain)
    act_two = normed_two.astype(jnp.bfloat16)
    gate = jnp.dot(act_two, w_gate, preferred_element_type=jnp.float32)
    up_proj = jnp.dot(act_two, w_up, preferred_element_type=jnp.float32)
    units_full, pull_units = jax.vjp(swiglu, gate, up_proj)
    hidden_units = units_full.astype(jnp.bfloat16)
    partial_ffn = jnp.dot(hidden_units, w_down, preferred_element_type=jnp.float32)
    output = (hidden_state + exchange_sum(partial_ffn)).astype(jnp.bfloat16)
    half = hidden_units.shape[1] // 2
    grad_down_a, grad_down_b = [
        scatter_sum(
            jnp.einsum("td,tf->df", cotangent, part, preferred_element_type=jnp.float32), order
        )
        for part, order in (
            (hidden_units[:, :half], X_FIRST),
            (hidden_units[:, half:], Y_FIRST),
        )
    ]
    grad_units = jnp.einsum("td,fd->tf", cotangent, w_down, preferred_element_type=jnp.float32)
    grad_gate_full, grad_up_full = pull_units(grad_units)
    grad_gate_lin = grad_gate_full.astype(jnp.bfloat16)
    grad_up_lin = grad_up_full.astype(jnp.bfloat16)
    grad_gate_w = jnp.einsum(
        "td,tf->df", act_two, grad_gate_lin, preferred_element_type=jnp.float32
    )
    grad_up_w = jnp.einsum("td,tf->df", act_two, grad_up_lin, preferred_element_type=jnp.float32)
    partial_two = jnp.einsum("tf,df->td", grad_gate_lin, w_gate, preferred_element_type=jnp.float32)
    partial_two = partial_two + jnp.einsum(
        "tf,df->td", grad_up_lin, w_up, preferred_element_type=jnp.float32
    )
    grad_act_two = exchange_sum(partial_two)
    grad_from_two, grad_ffn_gain = pull_two(grad_act_two)
    grad_hidden = grad_out + grad_from_two
    grad_attention = grad_hidden.astype(jnp.bfloat16)
    grad_out_w = jnp.einsum("td,tc->dc", grad_attention, mixed, preferred_element_type=jnp.float32)
    grad_query_lin, grad_key_lin, grad_value_lin, partial_one = attention_backward(
        branch_point, grad_attention, queries, keys, values, log_sums,
        w_out, w_query, w_key, w_value, rope,
    )
    grad_query_w = jnp.einsum(
        "td,tc->dc", act_one, grad_query_lin, preferred_element_type=jnp.float32
    )
    grad_key_w = jnp.einsum("td,tc->dc", act_one, grad_key_lin, preferred_element_type=jnp.float32)
    grad_value_w = jnp.einsum(
        "td,tc->dc", act_one, grad_value_lin, preferred_element_type=jnp.float32
    )
    grad_act_one = exchange_sum(partial_one)
    grad_from_one, grad_attn_gain = pull_one(grad_act_one)
    grad_input = (grad_hidden + grad_from_one).astype(jnp.bfloat16)
    rows = grad_attn_gain.shape[0] // lax.axis_size("dp")
    gains = lax.psum(jnp.stack([grad_attn_gain, grad_ffn_gain]), "dp")
    gains = lax.dynamic_slice_in_dim(gains, lax.axis_index("dp") * rows, rows, axis=1)
    return (
        output,
        grad_input,
        gains[0],
        scatter_sum(grad_query_w, Y_FIRST),
        scatter_sum(grad_key_w, X_FIRST),
        scatter_sum(grad_value_w, X_FIRST),
        scatter_sum(grad_out_w, X_FIRST).T,
        gains[1],
        scatter_sum(grad_gate_w, X_FIRST),
        scatter_sum(grad_up_w, Y_FIRST),
        jnp.concatenate([grad_down_a.T, grad_down_b.T], axis=0),
    )


def solution(mesh):
    placed = (
        P("dp", None),
        P("dp", None),
        P(),
        P(None, "tensor"),
        P(None, "tensor"),
        P(None, "tensor"),
        P("tensor", None),
        P(),
        P(None, "tensor"),
        P(None, "tensor"),
        P("tensor", None),
        P("dp", None),
    )
    return jax.shard_map(
        per_device,
        mesh=mesh,
        in_specs=placed,
        out_specs=(
            P("dp", None),
            P("dp", None),
            P("dp"),
            P("dp", "tensor"),
            P("dp", "tensor"),
            P("dp", "tensor"),
            P("tensor", "dp"),
            P("dp"),
            P("dp", "tensor"),
            P("dp", "tensor"),
            P("tensor", "dp"),
        ),
        check_vma=False,
    )
```

time: 1020 us -> 682 us (0.67)
  matrix products: 357 us -> 140 us
  local copies, waits for them, and re-layouts: 167 us -> 32.4 us
  other arithmetic: 153 us -> 61.2 us
  Pallas kernels: 0 us -> 89.8 us
  blocking collectives: 0 us -> 74.9 us
  waiting for transfers between devices: 273 us -> 240 us
  starting transfers between devices: 43.1 us -> 29.3 us
    dot_general x22 -> x0, matrix products: 209 us -> none  [the longest x4 66.2 us: block_scores(): jnp.einsum('qkgd,pkd->kgqp', query_block, keys, preferred_element_type=jn...]
    unnamed x2 -> x0, waiting for transfers between devices: 112 us -> none
    pallas_call x0 -> x2, Pallas kernels: none -> 89.8 us  [the longest x1 49.8 us: attention_backward(): pl.pallas_call(attention_backward_kernel, out_shape=(jax.ShapeDtypeStruct...]
    dynamic_update_slice x4 -> x0, local copies, waits for them, and re-layouts: 83.9 us -> none  [per_device(): mixed, log_totals = lax.map(forward_block, (queries, allowed_blocks))]
    ppermute x32, waiting for transfers between devices: 161 us -> 240 us  [scatter_sum(): received = lax.ppermute(sent, 'dp', pairs)]
    psum x0 -> x1, blocking collectives: none -> 74.9 us  [per_device(): gains = lax.psum(jnp.stack([grad_attn_gain, grad_ffn_gain]), 'dp')]
    convert_element_type x4 -> x1, other arithmetic: 44.5 us -> 4.47 us  [per_device(): grad_attention = grad_hidden.astype(jnp.bfloat16)]
    reduce_sum x3 -> x0, other arithmetic: 27.7 us -> none  [the longest x2 26.8 us: forward_block(): totals = jnp.sum(shifted, axis=-1, keepdims=True)]
  transfers between devices with their start and end apart: 37 -> 36, of which waited for: 18 -> 21; matrix products, arithmetic and copies ran while one was open for 46% -> 18% of each run, Pallas kernels for 0% -> 7%
where the time goes in v2:
time: 682 us; the launch traced here: 674 us
  waiting for transfers between devices  240 us (35%)
  matrix products  140 us (21%)
  Pallas kernels  89.8 us (13%)
  blocking collectives  74.9 us (11%)
  other arithmetic  61.2 us (9%)
  local copies, waits for them, and re-layouts  32.4 us (5%)
  starting transfers between devices  29.3 us (4%)
    ppermute x32, waiting for transfers between devices, scatter_sum(): received = lax.ppermute(sent, 'dp', pairs)  240 us
    psum x1, blocking collectives, per_device(): gains = lax.psum(jnp.stack([grad_attn_gain, grad_ffn_gain]), 'dp')  74.9 us
    pallas_call x1, Pallas kernels, attention_backward(): pl.pallas_call(attention_backward_kernel, out_shape=(jax.ShapeDtypeStruct...  49.8 us
    pallas_call x1, Pallas kernels, attention_forward(): pl.pallas_call(attention_forward_kernel, out_shape=(jax.ShapeDtypeStruct(...  40 us
    ppermute x32, starting transfers between devices, scatter_sum(): received = lax.ppermute(sent, 'dp', pairs)  28.7 us
    dot_general x1, matrix products, per_device(): gate = jnp.dot(act_two, w_gate, preferred_element_type=jnp.float32)  23.7 us
    convert_element_type x1, other arithmetic, per_device(): grad_input = (grad_hidden + grad_from_one).astype(jnp.bfloat16)  18.5 us
    convert_element_type x24, other arithmetic, scatter_sum(): work = total.astype(jnp.bfloat16) if left else total  18 us
  transfers between devices with their start and end apart: 36, of which 21 were waited for; matrix products, arithmetic and copies ran while one was open for 18% of the time, Pallas kernels for 7%

profile of v2, /device:TPU:0, one launch (start us, length us, event | category | flops | bytes accessed | tf_op | source)
XLA Modules:
  0.0 673.7 jit_solution(14014674836455708246)
XLA Ops:
  10.5 40.0 %attention_forward.1 = (bf16[1280,1536]{1,0:T(8,128)(2,1)}, bf16[4,5,512,128]{3,2,1,0:T(8,128)(2,1)}, bf16[4,1280,128]{2,1,0:T(8,128)(2,1)}, bf16[4,1280,128]{2,...) custom-call(s32[1,2]{1,0:T(1,128)} %branch_ref.3, ...), custom_call_target="tpu_custom_call" | custom-call | flops 20000000000 | bytes 40000000 | tf_op jit(solution)/shard_map/attention_forward/pallas_call | solution.py:171
  51.0 14.0 %fusion.50 = f32[1280,2048]{1,0:T(8,128)} fusion(bf16[1280,1536]{1,0:T(8,128)(2,1)} %param.24, bf16[2048,1536]{1,0:T(8,128)(2,1)} %param.23), kind=kOutput, calls=%fused_computation.175 | convolution fusion | flops 8053063680 | bytes 20709376 | tf_op jit(solution)/shard_map/td,fd->tf/dot_general | solution.py:381
  74.9 11.7 %fusion.49 = f32[1280,2048]{1,0:T(8,128)} fusion(bf16[1280,1536]{1,0:T(8,128)(2,1)S(1)} %multiply_convert_fusion.2, bf16[1536,2048]{1,0:T(8,128)(2,1)S(1)} %bitcast.252), kind=kOutput, calls=%fused_computation.174 | convolution fusion | flops 8053063680 | bytes 20709376 | tf_op jit(solution)/shard_map/dot_general | solution.py:366
  86.5 23.7 %multiply_convert_fusion = (bf16[1280,2048]{1,0:T(8,128)(2,1)}, bf16[1280,2048]{1,0:T(8,128)(2,1)}, bf16[1280,2048]{1,0:T(8,128)(2,1)}) fusion(f32[1280,2048]{1,0:T(8,128)} %fusion.50, f32[1280,2048]{1,0:T(8,128)} %fusion.49, bf16[1280,1536]{1,0:T(8,128)(2,1)} %copy-done.13, bf16[1536,2048]{1,0:T(8,128)(2,1)} %param.21), kind=kOutput, calls=%fused_computation.11 | convolution fusion | flops 8095006720 | bytes 46923776 | tf_op jit(solution)/shard_map/dot_general | solution.py:365
  110.3 9.0 %fusion.16 = bf16[1536,1024]{0,1:T(8,128)(2,1)} fusion(bf16[1280,1536]{1,0:T(8,128)(2,1)} %param.24, bf16[1280,2048]{1,0:T(8,128)(2,1)} %get-tuple-element.41), kind=kOutput, calls=%fused_computation.44 | convolution fusion | flops 4028104704 | bytes 9699328 | tf_op jit(solution)/shard_map/td,tf->df/dot_general | solution.py:374
  125.2 10.5 %convolution_convert_fusion.1 = bf16[1536,2048]{1,0:T(8,128)(2,1)} fusion(bf16[1280,1536]{1,0:T(8,128)(2,1)S(1)} %copy-done.14, bf16[1280,2048]{1,0:T(8,128)(2,1)S(1)} %bitcast.254), kind=kOutput, calls=%fused_computation.32 | convolution fusion | flops 8056209408 | bytes 15466496 | tf_op jit(solution)/shard_map/td,tf->df/dot_general | solution.py:385
  135.6 10.8 %fusion.51 = f32[1280,1536]{1,0:T(8,128)} fusion(bf16[1280,2048]{1,0:T(8,128)(2,1)S(1)} %bitcast.254, bf16[1536,2048]{1,0:T(8,128)(2,1)S(1)} %bitcast.250), kind=kOutput, calls=%fused_computation.176 | convolution fusion | flops 8053063680 | bytes 19398656 | tf_op jit(solution)/shard_map/tf,df->td/dot_general | solution.py:389
  164.7 10.3 %convolution_convert_fusion = bf16[1536,2048]{1,0:T(8,128)(2,1)S(1)} fusion(bf16[1280,1536]{1,0:T(8,128)(2,1)S(1)} %copy-done.15, bf16[1280,2048]{1,0:T(8,128)(2,1)} %get-tuple-element.39), kind=kOutput, calls=%fused_computation.31 | convolution fusion | flops 8056209408 | bytes 15466496 | tf_op jit(solution)/shard_map/td,tf->df/dot_general | solution.py:388
  181.2 13.7 %convolution_convert_fusion.2 = bf16[1280,1536]{1,0:T(8,128)(2,1)} fusion(bf16[1280,2048]{1,0:T(8,128)(2,1)} %get-tuple-element.41, bf16[2048,1536]{1,0:T(8,128)(2,1)} %param.23), kind=kOutput, calls=%fused_computation.33 | convolution fusion | flops 8055029760 | bytes 15466496 | tf_op jit(solution)/shard_map/dot_general | solution.py:369
  202.9 13.2 %fusion.11 = bf16[1280,1536]{1,0:T(8,128)(2,1)S(1)} fusion(f32[1280,1536]{1,0:T(8,128)} %fusion.51, bf16[1280,2048]{1,0:T(8,128)(2,1)} %get-tuple-element.39, bf16[1536,2048]{1,0:T(8,128)(2,1)} %param.22), kind=kOutput, calls=%fused_computation.30 | convolution fusion | flops 8056995840 | bytes 23330816 | tf_op jit(solution)/shard_map/tf,df->td/dot_general | solution.py:390
  216.2 67.9 %collective-permute-done.29 = bf16[2,2,96,1024]{3,2,1,0:T(8,128)(2,1)S(1)} collective-permute-done((bf16[2,2,96,1024]{3,2,1,0:T(8,128)(2,1)S(1)}, bf16[2,2,96,1024]{3,2,1,0:T(8,128)(2,1)S(1)}, u32[]{:S(2)}, u32[]{:S(2)}) %collective-permute-start.29) | collective-permute-done | bytes 786464 | tf_op jit(solution)/shard_map/ppermute | solution.py:330
  287.0 9.6 %collective-permute-done.30 = bf16[2,96,1024]{2,1,0:T(8,128)(2,1)S(1)} collective-permute-done((bf16[2,96,1024]{2,1,0:T(8,128)(2,1)S(1)}, bf16[2,96,1024]{2,1,0:T(8,128)(2,1)S(1)}, u32[]{:S(2)}, u32[]{:S(2)}) %collective-permute-start.30) | collective-permute-done | bytes 393248 | tf_op jit(solution)/shard_map/ppermute | solution.py:330
  306.1 7.6 %collective-permute-done.31 = bf16[96,1024]{1,0:T(8,128)(2,1)S(1)} collective-permute-done((bf16[96,1024]{1,0:T(8,128)(2,1)S(1)}, bf16[96,1024]{1,0:T(8,128)(2,1)S(1)}, u32[]{:S(2)}, u32[]{:S(2)}) %collective-permute-start.31) | collective-permute-done | bytes 196640 | tf_op jit(solution)/shard_map/ppermute | solution.py:330
  313.8 10.8 %collective-permute-done.35 = bf16[96,1024]{1,0:T(8,128)(2,1)S(1)} collective-permute-done((bf16[96,1024]{1,0:T(8,128)(2,1)S(1)}, bf16[96,1024]{1,0:T(8,128)(2,1)S(1)}, u32[]{:S(2)}, u32[]{:S(2)}) %collective-permute-start.35) | collective-permute-done | bytes 196640 | tf_op jit(solution)/shard_map/ppermute | solution.py:330
  345.1 6.8 %convolution_convert_fusion.5 = bf16[1536,768]{1,0:T(8,128)(2,1)} fusion(bf16[1280,1536]{1,0:T(8,128)(2,1)} %fusion.47.gatt_ref, bf16[1280,768]{1,0:T(8,128)(2,1)S(1)} %copy-done.28), kind=kOutput, calls=%fused_computation.42 | convolution fusion | flops 3021078528 | bytes 8257536 | tf_op jit(solution)/shard_map/td,tc->dc/dot_general | solution.py:397
  351.9 49.8 %attention_backward.1 = (bf16[1280,768]{1,0:T(8,128)(2,1)}, bf16[1280,384]{1,0:T(8,128)(2,1)}, bf16[1280,384]{1,0:T(8,128)(2,1)}, bf16[1280,1536]{1,0:T(8,128)(2,1)}) custom-call(s32[1,2]{1,0:T(1,128)} %branch_ref.3, bf16[1280,1536]{1,0:T(8,128)(2,1)} %fusion.47.gatt_ref, bf16[4,5,512,128]{3,2,1,0:T(8,128)(2,1)} %get-tuple-element.23.q_ref, ...), custom_call_target="tpu_custom_call" | custom-call | flops 35000000512 | bytes 40000000 | tf_op jit(solution)/shard_map/attention_backward/pallas_call | solution.py:278
  415.7 9.8 %collective-permute-done.12 = bf16[2,2,2,96,384]{4,3,0,1,2:T(8,128)(2,1)S(1)} collective-permute-done((bf16[2,2,2,96,384]{4,3,0,1,2:T(8,128)(2,1)S(1)}, bf16[2,2,2,96,384]{4,3,0,1,2:T(8,128)(2,1)S(1)}, u32[]{:S(2)}, u32[]{:S(2)}) %collective-permute-start.12) | collective-permute-done | bytes 589856 | tf_op jit(solution)/shard_map/ppermute | solution.py:330
  426.8 11.2 %collective-permute-done.8 = bf16[2,2,2,96,384]{4,3,0,1,2:T(8,128)(2,1)S(1)} collective-permute-done((bf16[2,2,2,96,384]{4,3,0,1,2:T(8,128)(2,1)S(1)}, bf16[2,2,2,96,384]{4,3,0,1,2:T(8,128)(2,1)S(1)}, u32[]{:S(2)}, u32[]{:S(2)}) %collective-permute-start.8) | collective-permute-done | bytes 589856 | tf_op jit(solution)/shard_map/ppermute | solution.py:330
  444.7 25.3 %collective-permute-done.13 = bf16[2,2,96,384]{3,2,0,1:T(8,128)(2,1)S(1)} collective-permute-done((bf16[2,2,96,384]{3,2,0,1:T(8,128)(2,1)S(1)}, bf16[2,2,96,384]{3,2,0,1:T(8,128)(2,1)S(1)}, u32[]{:S(2)}, u32[]{:S(2)}) %collective-permute-start.13) | collective-permute-done | bytes 294944 | tf_op jit(solution)/shard_map/ppermute | solution.py:330
  503.9 13.8 %collective-permute-done.26 = bf16[2,96,2048]{2,1,0:T(8,128)(2,1)S(1)} collective-permute-done((bf16[2,96,2048]{2,1,0:T(8,128)(2,1)S(1)}, bf16[2,96,2048]{2,1,0:T(8,128)(2,1)S(1)}, u32[]{:S(2)}, u32[]{:S(2)}) %collective-permute-start.26) | collective-permute-done | bytes 786464 | tf_op jit(solution)/shard_map/ppermute | solution.py:330
  518.1 21.6 %collective-permute-done.22 = bf16[2,96,2048]{2,1,0:T(8,128)(2,1)S(1)} collective-permute-done((bf16[2,96,2048]{2,1,0:T(8,128)(2,1)S(1)}, bf16[2,96,2048]{2,1,0:T(8,128)(2,1)S(1)}, u32[]{:S(2)}, u32[]{:S(2)}) %collective-permute-start.22) | collective-permute-done | bytes 786464 | tf_op jit(solution)/shard_map/ppermute | solution.py:330
  543.5 16.4 %collective-permute-done.27 = bf16[96,2048]{1,0:T(8,128)(2,1)S(1)} collective-permute-done((bf16[96,2048]{1,0:T(8,128)(2,1)S(1)}, bf16[96,2048]{1,0:T(8,128)(2,1)S(1)}, u32[]{:S(2)}, u32[]{:S(2)}) %collective-permute-start.27) | collective-permute-done | bytes 393248 | tf_op jit(solution)/shard_map/ppermute | solution.py:330
  579.2 74.9 %psum.7 = f32[2,1536]{1,0:T(2,128)S(1)} all-reduce(f32[2,1536]{1,0:T(2,128)S(1)} %pad_maximum_fusion.2), channel_id=1, replica_groups=mesh['dp'=16,'tensor'=2] {'dp'}, use_global_device_ids=true, to_apply=%region_6.7 | all-reduce | flops 3072 | bytes 24576 | tf_op jit(solution)/shard_map/psum | solution.py:413
  654.8 18.5 %fusion.6 = (bf16[1280,1536]{1,0:T(8,128)(2,1)}, bf16[1280,1536]{1,0:T(8,128)(2,1)}) fusion(bf16[1280,1536]{1,0:T(8,128)(2,1)} %x_ref.1, bf16[1280,1536]{1,0:T(8,128)(2,1)} %copy-done.8, bf16[1280,1536]{1,0:T(8,128)(2,1)} %get-tuple-element.27, f32[1280]{0:T(1024)S(1)} %multiply_multiply_fusion, f32[1280]{0:T(1024)S(1)} %fusion.46, f32[1536]{0:T(1024)S(1)} %copy-done.24, ...), kind=kLoop, calls=%fused_computation.18 | loop fusion | flops 51118080 | bytes 47218688 | tf_op jit(solution)/shard_map/convert_element_type | solution.py:411
  (242 shorter events, 167.0 us)
Async XLA Ops:
  151.2 43.7 %collective-permute-start.28 = (bf16[2,2,2,96,1024]{4,3,2,1,0:T(8,128)(2,1)}, bf16[2,2,2,96,1024]{4,3,2,1,0:T(8,128)(2,1)}, u32[]{:S(2)}, u32[]{:S(2)}) collective-permute-start(bf16[2,2,2,96,1024]{4,3,2,1,0:T(8,128)(2,1)} %dynamic-slice_bitcast_fusion), channel_id=1, source_target_pairs={{0,2},{2,0},{4,6},{6,4},{8,10},{10,8},{12,14},{14,12},{16,18},{18,... | collective-permute-start | bytes 4718600 | tf_op jit(solution)/shard_map/ppermute | solution.py:330
  163.1 37.5 %collective-permute-start.32 = (bf16[2,2,2,96,1024]{4,3,0,1,2:T(8,128)(2,1)}, bf16[2,2,2,96,1024]{4,3,0,1,2:T(8,128)(2,1)}, u32[]{:S(2)}, u32[]{:S(2)}) collective-permute-start(bf16[2,2,2,96,1024]{4,3,0,1,2:T(8,128)(2,1)} %bitcast.226), channel_id=1, source_target_pairs={{0,4},{2,6},{4,0},{6,2},{8,12},{10,14},{12,8},{14,10},{16,20},{18,... | collective-permute-start | bytes 4718600 | tf_op jit(solution)/shard_map/ppermute | solution.py:330
  176.4 149.2 %collective-permute-start.24 = (bf16[2,2,2,96,2048]{4,3,0,1,2:T(8,128)(2,1)S(1)}, bf16[2,2,2,96,2048]{4,3,0,1,2:T(8,128)(2,1)}, u32[]{:S(2)}, u32[]{:S(2)}) collective-permute-start(bf16[2,2,2,96,2048]{4,3,0,1,2:T(8,128)(2,1)S(1)} %bitcast.240), channel_id=1, source_target_pairs={{0,4},{2,6},{4,0},{6,2},{8,12},{10,14},{12,8},{14,10},{16,20},{18,... | collective-permute-start | bytes 9437192 | tf_op jit(solution)/shard_map/ppermute | solution.py:330
  180.7 151.0 %collective-permute-start.20 = (bf16[2,2,2,96,2048]{4,3,0,1,2:T(8,128)(2,1)}, bf16[2,2,2,96,2048]{4,3,0,1,2:T(8,128)(2,1)}, u32[]{:S(2)}, u32[]{:S(2)}) collective-permute-start(bf16[2,2,2,96,2048]{4,3,0,1,2:T(8,128)(2,1)} %bitcast.225), channel_id=1, source_target_pairs={{0,2},{2,0},{4,6},{6,4},{8,10},{10,8},{12,14},{14,12},{16,18},{18,... | collective-permute-start | bytes 9437192 | tf_op jit(solution)/shard_map/ppermute | solution.py:330
  197.2 86.9 %collective-permute-start.29 = (bf16[2,2,96,1024]{3,2,1,0:T(8,128)(2,1)S(1)}, bf16[2,2,96,1024]{3,2,1,0:T(8,128)(2,1)S(1)}, u32[]{:S(2)}, u32[]{:S(2)}) collective-permute-start(bf16[2,2,96,1024]{3,2,1,0:T(8,128)(2,1)S(1)} %dynamic-slice_bitcast_fusion.4), channel_id=1, source_target_pairs={{0,4},{2,6},{4,0},{6,2},{8,12},{10,14},{12,8},{14,10},{16,20},{18,... | collective-permute-start | bytes 2359304 | tf_op jit(solution)/shard_map/ppermute | solution.py:330
  202.8 83.3 %collective-permute-start.33 = (bf16[2,2,96,1024]{3,2,0,1:T(8,128)(2,1)S(1)}, bf16[2,2,96,1024]{3,2,0,1:T(8,128)(2,1)S(1)}, u32[]{:S(2)}, u32[]{:S(2)}) collective-permute-start(bf16[2,2,96,1024]{3,2,0,1:T(8,128)(2,1)S(1)} %dynamic-slice_bitcast_fusion.3), channel_id=1, source_target_pairs={{0,2},{2,0},{4,6},{6,4},{8,10},{10,8},{12,14},{14,12},{16,18},{18,... | collective-permute-start | bytes 2359304 | tf_op jit(solution)/shard_map/ppermute | solution.py:330
  216.2 121.1 %collective-permute-start.2 = (bf16[1280,1536]{1,0:T(8,128)(2,1)S(1)}, bf16[1280,1536]{1,0:T(8,128)(2,1)S(1)}, u32[]{:S(2)}, u32[]{:S(2)}) collective-permute-start(bf16[1280,1536]{1,0:T(8,128)(2,1)S(1)} %fusion.11), channel_id=1, source_target_pairs={{0,1},{1,0},{2,3},{3,2},{4,5},{5,4},{6,7},{7,6},{8,9},{9,8},{10,11... | collective-permute-start | bytes 11796488 | tf_op jit(solution)/shard_map/ppermute | solution.py:312
  286.5 16.9 %collective-permute-start.34 = (bf16[2,96,1024]{2,1,0:T(8,128)(2,1)S(1)}, bf16[2,96,1024]{2,1,0:T(8,128)(2,1)S(1)}, u32[]{:S(2)}, u32[]{:S(2)}) collective-permute-start(bf16[2,96,1024]{2,1,0:T(8,128)(2,1)S(1)} %dynamic-slice_bitcast_fusion.9), channel_id=1, source_target_pairs={{0,8},{2,10},{4,12},{6,14},{8,0},{10,2},{12,4},{14,6},{16,24},{18,... | collective-permute-start | bytes 1179656 | tf_op jit(solution)/shard_map/ppermute | solution.py:330
  296.6 358.2 %collective-permute-start.1 = (bf16[1280,1536]{1,0:T(8,128)(2,1)}, bf16[1280,1536]{1,0:T(8,128)(2,1)}, u32[]{:S(2)}, u32[]{:S(2)}) collective-permute-start(bf16[1280,1536]{1,0:T(8,128)(2,1)} %convolution_convert_fusion.2), channel_id=1, source_target_pairs={{0,1},{1,0},{2,3},{3,2},{4,5},{5,4},{6,7},{7,6},{8,9},{9,8},{10,11... | collective-permute-start | bytes 11796488 | tf_op jit(solution)/shard_map/ppermute | solution.py:312
  330.3 109.2 %collective-permute-start.25 = (bf16[2,2,96,2048]{3,2,0,1:T(8,128)(2,1)}, bf16[2,2,96,2048]{3,2,0,1:T(8,128)(2,1)}, u32[]{:S(2)}, u32[]{:S(2)}) collective-permute-start(bf16[2,2,96,2048]{3,2,0,1:T(8,128)(2,1)} %dynamic-slice_bitcast_fusion.1), channel_id=1, source_target_pairs={{0,2},{2,0},{4,6},{6,4},{8,10},{10,8},{12,14},{14,12},{16,18},{18,... | collective-permute-start | bytes 4718600 | tf_op jit(solution)/shard_map/ppermute | solution.py:330
  336.4 105.2 %collective-permute-start.21 = (bf16[2,2,96,2048]{3,2,0,1:T(8,128)(2,1)}, bf16[2,2,96,2048]{3,2,0,1:T(8,128)(2,1)}, u32[]{:S(2)}, u32[]{:S(2)}) collective-permute-start(bf16[2,2,96,2048]{3,2,0,1:T(8,128)(2,1)} %dynamic-slice_bitcast_fusion.2), channel_id=1, source_target_pairs={{0,4},{2,6},{4,0},{6,2},{8,12},{10,14},{12,8},{14,10},{16,20},{18,... | collective-permute-start | bytes 4718600 | tf_op jit(solution)/shard_map/ppermute | solution.py:330
  409.1 16.3 %collective-permute-start.12 = (bf16[2,2,2,96,384]{4,3,0,1,2:T(8,128)(2,1)S(1)}, bf16[2,2,2,96,384]{4,3,0,1,2:T(8,128)(2,1)S(1)}, u32[]{:S(2)}, u32[]{:S(2)}) collective-permute-start(bf16[2,2,2,96,384]{4,3,0,1,2:T(8,128)(2,1)S(1)} %bitcast.248), channel_id=1, source_target_pairs={{0,2},{2,0},{4,6},{6,4},{8,10},{10,8},{12,14},{14,12},{16,18},{18,... | collective-permute-start | bytes 1769480 | tf_op jit(solution)/shard_map/ppermute | solution.py:330
  410.4 27.6 %collective-permute-start.8 = (bf16[2,2,2,96,384]{4,3,0,1,2:T(8,128)(2,1)S(1)}, bf16[2,2,2,96,384]{4,3,0,1,2:T(8,128)(2,1)S(1)}, u32[]{:S(2)}, u32[]{:S(2)}) collective-permute-start(bf16[2,2,2,96,384]{4,3,0,1,2:T(8,128)(2,1)S(1)} %bitcast.247), channel_id=1, source_target_pairs={{0,2},{2,0},{4,6},{6,4},{8,10},{10,8},{12,14},{14,12},{16,18},{18,... | collective-permute-start | bytes 1769480 | tf_op jit(solution)/shard_map/ppermute | solution.py:330
  425.4 74.2 %collective-permute-start.16 = (bf16[2,2,2,96,768]{4,3,0,1,2:T(8,128)(2,1)S(1)}, bf16[2,2,2,96,768]{4,3,0,1,2:T(8,128)(2,1)S(1)}, u32[]{:S(2)}, u32[]{:S(2)}) collective-permute-start(bf16[2,2,2,96,768]{4,3,0,1,2:T(8,128)(2,1)S(1)} %bitcast.246), channel_id=1, source_target_pairs={{0,2},{2,0},{4,6},{6,4},{8,10},{10,8},{12,14},{14,12},{16,18},{18,... | collective-permute-start | bytes 3538952 | tf_op jit(solution)/shard_map/ppermute | solution.py:330
  438.1 63.7 %collective-permute-start.4 = (bf16[2,2,2,96,768]{4,3,0,1,2:T(8,128)(2,1)S(1)}, bf16[2,2,2,96,768]{4,3,0,1,2:T(8,128)(2,1)S(1)}, u32[]{:S(2)}, u32[]{:S(2)}) collective-permute-start(bf16[2,2,2,96,768]{4,3,0,1,2:T(8,128)(2,1)S(1)} %bitcast.245), channel_id=1, source_target_pairs={{0,4},{2,6},{4,0},{6,2},{8,12},{10,14},{12,8},{14,10},{16,20},{18,... | collective-permute-start | bytes 3538952 | tf_op jit(solution)/shard_map/ppermute | solution.py:330
  439.5 136.4 %collective-permute-start.3 = (bf16[1280,1536]{1,0:T(8,128)(2,1)S(1)}, bf16[1280,1536]{1,0:T(8,128)(2,1)S(1)}, u32[]{:S(2)}, u32[]{:S(2)}) collective-permute-start(bf16[1280,1536]{1,0:T(8,128)(2,1)S(1)} %copy-done.7), channel_id=1, source_target_pairs={{0,1},{1,0},{2,3},{3,2},{4,5},{5,4},{6,7},{7,6},{8,9},{9,8},{10,11... | collective-permute-start | bytes 11796488 | tf_op jit(solution)/shard_map/ppermute | solution.py:312
  441.6 28.4 %collective-permute-start.13 = (bf16[2,2,96,384]{3,2,0,1:T(8,128)(2,1)S(1)}, bf16[2,2,96,384]{3,2,0,1:T(8,128)(2,1)S(1)}, u32[]{:S(2)}, u32[]{:S(2)}) collective-permute-start(bf16[2,2,96,384]{3,2,0,1:T(8,128)(2,1)S(1)} %dynamic-slice_bitcast_fusion.14), channel_id=1, source_target_pairs={{0,4},{2,6},{4,0},{6,2},{8,12},{10,14},{12,8},{14,10},{16,20},{18,... | collective-permute-start | bytes 884744 | tf_op jit(solution)/shard_map/ppermute | solution.py:330
  498.7 19.1 %collective-permute-start.26 = (bf16[2,96,2048]{2,1,0:T(8,128)(2,1)S(1)}, bf16[2,96,2048]{2,1,0:T(8,128)(2,1)S(1)}, u32[]{:S(2)}, u32[]{:S(2)}) collective-permute-start(bf16[2,96,2048]{2,1,0:T(8,128)(2,1)S(1)} %dynamic-slice_bitcast_fusion.5), channel_id=1, source_target_pairs={{0,8},{2,10},{4,12},{6,14},{8,0},{10,2},{12,4},{14,6},{16,24},{18,... | collective-permute-start | bytes 2359304 | tf_op jit(solution)/shard_map/ppermute | solution.py:330
  499.6 40.1 %collective-permute-start.22 = (bf16[2,96,2048]{2,1,0:T(8,128)(2,1)S(1)}, bf16[2,96,2048]{2,1,0:T(8,128)(2,1)S(1)}, u32[]{:S(2)}, u32[]{:S(2)}) collective-permute-start(bf16[2,96,2048]{2,1,0:T(8,128)(2,1)S(1)} %dynamic-slice_bitcast_fusion.6), channel_id=1, source_target_pairs={{0,8},{2,10},{4,12},{6,14},{8,0},{10,2},{12,4},{14,6},{16,24},{18,... | collective-permute-start | bytes 2359304 | tf_op jit(solution)/shard_map/ppermute | solution.py:330
  501.8 38.3 %collective-permute-start.17 = (bf16[2,2,96,768]{3,2,0,1:T(8,128)(2,1)S(1)}, bf16[2,2,96,768]{3,2,0,1:T(8,128)(2,1)S(1)}, u32[]{:S(2)}, u32[]{:S(2)}) collective-permute-start(bf16[2,2,96,768]{3,2,0,1:T(8,128)(2,1)S(1)} %dynamic-slice_bitcast_fusion.7), channel_id=1, source_target_pairs={{0,4},{2,6},{4,0},{6,2},{8,12},{10,14},{12,8},{14,10},{16,20},{18,... | collective-permute-start | bytes 1769480 | tf_op jit(solution)/shard_map/ppermute | solution.py:330
  517.8 25.5 %collective-permute-start.5 = (bf16[2,2,96,768]{3,2,0,1:T(8,128)(2,1)S(1)}, bf16[2,2,96,768]{3,2,0,1:T(8,128)(2,1)S(1)}, u32[]{:S(2)}, u32[]{:S(2)}) collective-permute-start(bf16[2,2,96,768]{3,2,0,1:T(8,128)(2,1)S(1)} %dynamic-slice_bitcast_fusion.8), channel_id=1, source_target_pairs={{0,2},{2,0},{4,6},{6,4},{8,10},{10,8},{12,14},{14,12},{16,18},{18,... | collective-permute-start | bytes 1769480 | tf_op jit(solution)/shard_map/ppermute | solution.py:330
  539.7 20.2 %collective-permute-start.27 = (bf16[96,2048]{1,0:T(8,128)(2,1)S(1)}, bf16[96,2048]{1,0:T(8,128)(2,1)S(1)}, u32[]{:S(2)}, u32[]{:S(2)}) collective-permute-start(bf16[96,2048]{1,0:T(8,128)(2,1)S(1)} %dynamic-slice_bitcast_fusion.11), channel_id=1, source_target_pairs={{0,16},{2,18},{4,20},{6,22},{8,24},{10,26},{12,28},{14,30},{16,0},... | collective-permute-start | bytes 1179656 | tf_op jit(solution)/shard_map/ppermute | solution.py:330
  540.0 24.1 %collective-permute-start.23 = (bf16[96,2048]{1,0:T(8,128)(2,1)S(1)}, bf16[96,2048]{1,0:T(8,128)(2,1)S(1)}, u32[]{:S(2)}, u32[]{:S(2)}) collective-permute-start(bf16[96,2048]{1,0:T(8,128)(2,1)S(1)} %dynamic-slice_bitcast_fusion.12), channel_id=1, source_target_pairs={{0,16},{2,18},{4,20},{6,22},{8,24},{10,26},{12,28},{14,30},{16,0},... | collective-permute-start | bytes 1179656 | tf_op jit(solution)/shard_map/ppermute | solution.py:330
  543.2 21.9 %collective-permute-start.18 = (bf16[2,96,768]{2,1,0:T(8,128)(2,1)S(1)}, bf16[2,96,768]{2,1,0:T(8,128)(2,1)S(1)}, u32[]{:S(2)}, u32[]{:S(2)}) collective-permute-start(bf16[2,96,768]{2,1,0:T(8,128)(2,1)S(1)} %dynamic-slice_bitcast_fusion.13), channel_id=1, source_target_pairs={{0,8},{2,10},{4,12},{6,14},{8,0},{10,2},{12,4},{14,6},{16,24},{18,... | collective-permute-start | bytes 884744 | tf_op jit(solution)/shard_map/ppermute | solution.py:330
  (52 other events, 686.9 us)
